TPU v7x, 128 devices: a whole 4x4x4 slice. The times are simulated.
128 devices in a mesh: sec: 4 (over x_hi, core), region: 32 (over y, x_lo, z).
Axes of the slice: x: 4 (x_hi: 2, x_lo: 2; x = x_hi * 2 + x_lo), y: 4, z: 4, core: 2. Of those that a mesh axis runs over, the one named last changes fastest.
Arguments:
- windows: bfloat16 [4, 1536, 25600], P('sec', 'region'), may hold values from -24 to 24
- partner_dev: int32 [1536], P('region'), may hold values from 0 to 31, as said below
- partner_slot: int32 [1536], P('region'), may hold values from 0 to 47
Outputs:
- montage_flow: float32 [4, 2, 1536], P('sec', None, 'region')
- section_flow: float32 [4, 2, 1536], P('sec', None, 'region')
- displacement: float32 [4, 2, 1536], P('sec', None, 'region')
Inputs may be any that keep to these rules, and one draw needn't show every extreme that they name: The pairing is symmetric: the partner of window j is window partner_dev[j] * 48 + partner_slot[j], and that window's partner is j; the same pairing holds in every section. No window's partner lies on its own device, and for every two devices either none or exactly 3 of one device's windows have partners on the other.
All inputs are finite; a program needn't handle non-finite values.
Results may differ from a plain program's by a relative error of at most 0.00038.
Values may be sent and summed in bfloat16 or wider, within the bound.
A program may use at most 128 MiB of HBM per device.

v0:
```python
import math

import jax
import jax.numpy as jnp
from jax import lax
from jax.sharding import PartitionSpec as P

WIN = 160
RADIUS = 16
SHIFTS = 33
ITERS = 32


sharpness = 12.0
montage_stiffness = 1.0
section_stiffness = 1.0
anchor_stiffness = 0.05
step_length = 0.2


def shifted(block, axis, distance):
    devices = range(lax.axis_size(axis))
    route = [(i - distance, i) for i in devices if i - distance in devices]
    return lax.ppermute(block, axis, route)


def extended(array, sides, width):
    for axis, dim in sides:
        size, length = (lax.axis_size(axis), array.shape[dim])
        up = [(i, (i + 1) % size) for i in range(size - 1)]
        down = [(j, i) for i, j in up]
        last = lax.slice_in_dim(array, length - width, length, axis=dim)
        first = lax.slice_in_dim(array, 0, width, axis=dim)
        before = lax.ppermute(last, axis, up)
        after = lax.ppermute(first, axis, down)
        array = jnp.concatenate([before, array, after], axis=dim)
    return array


def dft_tables():
    indices = jnp.arange(WIN, dtype=jnp.int32)
    phase_index = indices[:, None] * indices[None, :] % WIN
    angles = phase_index.astype(jnp.float32) * (2.0 * math.pi / WIN)
    cosine_table = jnp.cos(angles).astype(jnp.bfloat16)
    sine_table = jnp.sin(angles).astype(jnp.bfloat16)
    offsets = jnp.arange(SHIFTS, dtype=jnp.int32) - RADIUS
    back_phase = offsets[:, None] * indices[None, :] % WIN
    back_angles = back_phase.astype(jnp.float32) * (2.0 * math.pi / WIN)
    back_cos = jnp.cos(back_angles).astype(jnp.bfloat16)
    back_sin = jnp.sin(back_angles).astype(jnp.bfloat16)
    return (cosine_table, sine_table, back_cos, back_sin, offsets)


def spectra_block(images, cosine_table, sine_table):
    window_count = images.shape[0]
    square = images.reshape(window_count, WIN, WIN)
    right_table = jnp.concatenate([cosine_table, -sine_table], axis=1)
    first_segment = jnp.einsum(
        "bxy,yk->bxk", square, right_table, preferred_element_type=jnp.float32
    ).astype(jnp.bfloat16)
    left_table = jnp.concatenate([cosine_table, sine_table], axis=0)
    products = jnp.einsum(
        "kx,bxj->bkj", left_table, first_segment, preferred_element_type=jnp.float32
    )
    spec_real = products[:, :WIN, :WIN] + products[:, WIN:, WIN:]
    spec_imag = products[:, :WIN, WIN:] - products[:, WIN:, :WIN]
    return jnp.concatenate([spec_real, spec_imag], axis=2).astype(jnp.bfloat16)


def spectra_all(images, cosine_table, sine_table):
    window_count = images.shape[0]
    grouped = images.reshape(window_count // 8, 8, WIN * WIN)
    result = lax.map(lambda members: spectra_block(members, cosine_table, sine_table), grouped)
    return result.reshape(window_count, WIN, 2 * WIN)


def spectral_energy(spectrum):
    values = spectrum.astype(jnp.float32)
    return jnp.sum(values * values, axis=(1, 2)) / (WIN * WIN)


def correlate_block(
    first_spec, second_spec, first_energy, second_energy, back_cos, back_sin, offsets
):
    first_real = first_spec[:, :, :WIN].astype(jnp.float32)
    first_imag = first_spec[:, :, WIN:].astype(jnp.float32)
    second_real = second_spec[:, :, :WIN].astype(jnp.float32)
    second_imag = second_spec[:, :, WIN:].astype(jnp.float32)
    cross_real = (first_real * second_real + first_imag * second_imag) / (WIN * WIN)
    cross_imag = (first_imag * second_real - first_real * second_imag) / (WIN * WIN)
    cross_power = jnp.concatenate([cross_real, cross_imag], axis=2).astype(jnp.bfloat16)
    back_left = jnp.concatenate([back_cos, back_sin], axis=0)
    partial_back = jnp.einsum(
        "sk,bkj->bsj", back_left, cross_power, preferred_element_type=jnp.float32
    )
    back_real = partial_back[:, :SHIFTS, :WIN] - partial_back[:, SHIFTS:, WIN:]
    back_imag = partial_back[:, :SHIFTS, WIN:] + partial_back[:, SHIFTS:, :WIN]
    half_back = jnp.concatenate([back_real, back_imag], axis=2).astype(jnp.bfloat16)
    back_right = jnp.concatenate([back_cos.T, -back_sin.T], axis=0)
    surface = jnp.einsum("bsj,jt->bst", half_back, back_right, preferred_element_type=jnp.float32)
    normed = surface / jnp.sqrt(first_energy * second_energy + 1e-06)[:, None, None]
    weights = jnp.exp(sharpness * normed)
    weight_total = jnp.sum(weights, axis=(1, 2))
    shift_values = offsets.astype(jnp.float32)
    row_flow = jnp.sum(weights * shift_values[None, :, None], axis=(1, 2)) / weight_total
    col_flow = jnp.sum(weights * shift_values[None, None, :], axis=(1, 2)) / weight_total
    return jnp.stack([row_flow, col_flow], axis=1)


def correlate_all(first_spec, second_spec, back_cos, back_sin, offsets):
    window_count = first_spec.shape[0]
    first_energy = spectral_energy(first_spec)
    second_energy = spectral_energy(second_spec)
    members = (
        first_spec.reshape(window_count // 8, 8, WIN, 2 * WIN),
        second_spec.reshape(window_count // 8, 8, WIN, 2 * WIN),
        first_energy.reshape(window_count // 8, 8),
        second_energy.reshape(window_count // 8, 8),
    )
    flows = lax.map(
        lambda parts: correlate_block(
            parts[0], parts[1], parts[2], parts[3], back_cos, back_sin, offsets
        ),
        members,
    )
    return flows.reshape(window_count, 2)


def body(windows, partner_dev, partner_slot):
    cosine_table, sine_table, back_cos, back_sin, offsets = dft_tables()
    own_windows = windows[0]
    window_count = own_windows.shape[0]
    regions = lax.axis_size("region")
    capacity = 2 * window_count // regions
    positions = jnp.arange(window_count, dtype=jnp.int32)
    same_target = partner_dev[:, None] == partner_dev[None, :]
    send_rank = jnp.sum(same_target & (partner_slot[None, :] < partner_slot[:, None]), axis=1)
    recv_rank = jnp.sum(same_target & (positions[None, :] < positions[:, None]), axis=1)
    send_index = partner_dev * capacity + send_rank
    recv_index = partner_dev * capacity + recv_rank
    section_index = lax.axis_index("sec")
    last_flag = section_index == lax.axis_size("sec") - 1
    outgoing = (
        jnp.zeros((regions * capacity, WIN * WIN), jnp.bfloat16)
        .at[send_index]
        .set(own_windows, mode="drop")
    )
    incoming = lax.all_to_all(
        outgoing.reshape(regions, capacity, WIN * WIN),
        "region",
        split_axis=0,
        concat_axis=0,
        tiled=True,
    )
    partner_windows = incoming.reshape(regions * capacity, WIN * WIN)[recv_index]
    following = shifted(own_windows, "sec", -1)
    own_spec = spectra_all(own_windows, cosine_table, sine_table)
    partner_spec = spectra_all(partner_windows, cosine_table, sine_table)
    next_spec = spectra_all(following, cosine_table, sine_table)
    montage = correlate_all(own_spec, partner_spec, back_cos, back_sin, offsets)
    section = correlate_all(own_spec, next_spec, back_cos, back_sin, offsets)
    section = jnp.where(last_flag, 0.0, section)
    previous_flow = shifted(section, "sec", 1)
    has_next = jnp.where(last_flag, 0.0, 1.0).astype(jnp.float32)
    has_prev = jnp.where(section_index > 0, 1.0, 0.0).astype(jnp.float32)
    flow_out = jnp.zeros((regions * capacity, 2), jnp.float32).at[send_index].set(montage)
    flow_in = lax.all_to_all(
        flow_out.reshape(regions, capacity, 2), "region", split_axis=0, concat_axis=0, tiled=True
    )
    partner_flow = flow_in.reshape(regions * capacity, 2)[recv_index]
    disagreement = montage - partner_flow

    def relax(turn_index, shift_field):
        field_out = jnp.zeros((regions * capacity, 2), jnp.float32).at[send_index].set(shift_field)
        field_in = lax.all_to_all(
            field_out.reshape(regions, capacity, 2),
            "region",
            split_axis=0,
            concat_axis=0,
            tiled=True,
        )
        partner_field = field_in.reshape(regions * capacity, 2)[recv_index]
        rims = extended(shift_field[None], (("sec", 0),), 1)
        previous_field = rims[0]
        next_field = rims[2]
        gradient = (
            montage_stiffness * (2.0 * shift_field - 2.0 * partner_field - disagreement)
            + section_stiffness * has_next * (shift_field - next_field - section)
            - section_stiffness * has_prev * (previous_field - shift_field - previous_flow)
            + anchor_stiffness * shift_field
        )
        return shift_field - step_length * gradient

    shift_field = lax.fori_loop(0, ITERS, relax, jnp.zeros((window_count, 2), jnp.float32))
    return (montage.T[None], section.T[None], shift_field.T[None])


def solution(mesh):
    placed = (P("sec", "region", None), P("region"), P("region"))
    return jax.shard_map(
        body,
        mesh=mesh,
        in_specs=placed,
        out_specs=(P("sec", None, "region"), P("sec", None, "region"), P("sec", None, "region")),
        check_vma=False,
    )
```

profile of v0, /device:TPU:1, one launch (start us, length us, event | category | flops | bytes accessed | tf_op | source)
XLA Modules:
  0.0 1095.3 jit_solution(27466597483328778)
XLA Ops:
  8.7 56.5 %while.79 = (s32[]{:T(128)}, bf16[6,8,160,320]{3,2,1,0:T(8,128)(2,1)}, bf16[6,8,25600]{2,1,0:T(8,128)(2,1)}, bf16[160,320]{1,0:T(8,128)(2,1)S(1)}, bf16[320,160]{0,1:T(8,128)(2,1)S(1)}) while((s32[]{:T(128)}, bf16[6,8,160,320]{3,2,1,0:T(8,128)(2,1)}, bf16[6,8,25600]{2,1,0:T(8,128)(2,1)}, bf16[160,320]{1,0:T(8,128)(2,1)S(1)}, ...), condition=%wide.region_1.2_spmd.clone, body=%wide.region_0.1_spmd.sunk.clone | while | flops 396083200 | bytes 11428417 | solution.py:73
  65.4 8.4 scatter_custom_fusion.1
  88.7 57.0 %while.81 = (s32[]{:T(128)}, bf16[6,8,160,320]{3,2,1,0:T(8,128)(2,1)}, bf16[6,8,25600]{2,1,0:T(8,128)(2,1)}, bf16[160,320]{1,0:T(8,128)(2,1)S(1)}, bf16[320,160]{0,1:T(8,128)(2,1)S(1)}) while((s32[]{:T(128)}, bf16[6,8,160,320]{3,2,1,0:T(8,128)(2,1)}, bf16[6,8,25600]{2,1,0:T(8,128)(2,1)}, bf16[160,320]{1,0:T(8,128)(2,1)S(1)}, ...), condition=%wide.region_15.16_spmd.clone, body=%wide.region_14.15_spmd.sunk.clone | while | flops 396083200 | bytes 11428417 | solution.py:73
  149.9 9.4 all-to-all-start.1
  159.2 24.0 %while.83 = (s32[]{:T(128)}, f32[6,8,2]{1,2,0:T(2,128)S(1)}, bf16[6,8,160,320]{3,2,1,0:T(8,128)(2,1)}, bf16[6,8,160,320]{3,2,1,0:T(8,128)(2,1)}, bf16[66,160]{1,...) while((s32[]{:T(128)}, f32[6,8,2]{1,2,0:T(2,128)S(1)}, ...), condition=%wide.region_21.22_spmd.clone.clone, body=%wide.region_17.21_spmd.clone.sunk.clone | while | flops 64716500 | bytes 8288497 | solution.py:120
  183.2 91.2 %all-to-all-done.1 = bf16[32,3,25600]{2,1,0:T(4,128)(2,1)} async-done(((bf16[32,3,25600]{2,1,0:T(4,128)(2,1)}), bf16[32,3,25600]{2,1,0:T(4,128)(2,1)}, u32[]{:S(2)}, u32[]{:S(2)}) %all-to-all-start.1) | async-done | bytes 4915232 | tf_op jit(solution)/shard_map/all_to_all | solution.py:148
  274.5 7.6 reshape.345
  282.0 8.6 gather_fusion.1
  293.8 57.1 %while.80 = (s32[]{:T(128)}, bf16[6,8,160,320]{3,2,1,0:T(8,128)(2,1)}, bf16[6,8,25600]{2,1,0:T(8,128)(2,1)}, bf16[160,320]{1,0:T(8,128)(2,1)S(1)}, bf16[320,160]{0,1:T(8,128)(2,1)S(1)}) while((s32[]{:T(128)}, bf16[6,8,160,320]{3,2,1,0:T(8,128)(2,1)}, bf16[6,8,25600]{2,1,0:T(8,128)(2,1)}, bf16[160,320]{1,0:T(8,128)(2,1)S(1)}, ...), condition=%wide.region_6.7_spmd.clone, body=%wide.region_5.6_spmd.sunk.clone | while | flops 396083200 | bytes 11428417 | solution.py:73
  355.1 24.2 %while.82 = (s32[]{:T(128)}, f32[6,8,2]{1,0,2:T(8,128)S(1)}, bf16[6,8,160,320]{3,2,1,0:T(8,128)(2,1)}, bf16[6,8,160,320]{3,2,1,0:T(8,128)(2,1)}, bf16[66,160]{1,...) while((s32[]{:T(128)}, f32[6,8,2]{1,0,2:T(8,128)S(1)}, ...), condition=%wide.region_13.14_spmd.clone.clone, body=%wide.region_9.13_spmd.clone.sunk.clone | while | flops 64716500 | bytes 8286705 | solution.py:120
  393.3 701.1 %while.84 = (s32[]{:T(128)}, f32[48,2]{1,0:T(8,128)S(1)}, s32[48]{0:T(128)S(1)}, s32[48]{0:T(128)S(1)}, f32[48,2]{1,0:T(8,128)S(1)}, /*index=5*/f32[]{:T(128)}, f32[48,2]{1,0:T(8,128)S(1)}, f32[]{:T(128)}, f32[48,2]{1,0:T(8,128)S(1)}) while((s32[]{:T(128)}, f32[48,2]{1,0:T(8,128)S(1)}, s32[48]{0:T(128)S(1)}, ...), condition=%wide.region_25.26_spmd.clone.clone, body=%wide.region_23.25_spmd.clone.sunk.clone | while | flops 3139 | bytes 116325 | solution.py:194
  393.5 7.5 collective-permute-start
  410.2 7.0 all-to-all-done
  418.2 7.2 collective-permute-start
  476.5 7.0 all-to-all-done
  498.3 7.0 all-to-all-done
  541.9 7.0 all-to-all-done
  563.7 7.0 all-to-all-done
  607.2 7.0 all-to-all-done
  629.0 7.0 all-to-all-done
  672.6 7.0 all-to-all-done
  694.4 7.0 all-to-all-done
  738.0 7.0 all-to-all-done
  759.8 7.0 all-to-all-done
  (965 shorter events, 872.9 us)
Async XLA Ops:
  0.6 84.9 %collective-permute-start.2 = (bf16[48,25600]{1,0:T(8,128)(2,1)}, bf16[48,25600]{1,0:T(8,128)(2,1)}, u32[]{:S(2)}, u32[]{:S(2)}) collective-permute-start(bf16[48,25600]{1,0:T(8,128)(2,1)} %bitcast.255), channel_id=1, source_target_pairs={{32,0},{64,32},{96,64},{33,1},{65,33},{97,65},{34,2},{66,34},{98,6... | collective-permute-start | bytes 7372808 | tf_op jit(solution)/shard_map/ppermute | solution.py:24
  149.9 124.6 %all-to-all-start.1 = ((bf16[32,3,25600]{2,1,0:T(4,128)(2,1)}), bf16[32,3,25600]{2,1,0:T(4,128)(2,1)}, u32[]{:S(2)}, u32[]{:S(2)}) async-start(bf16[32,3,25600]{2,1,0:T(4,128)(2,1)} %reshape.344), calls=%async_computation.1 | async-start | bytes 13107200 | tf_op jit(solution)/shard_map/all_to_all | solution.py:148
  393.5 16.6 %collective-permute-start = (f32[1,48,2]{1,2,0:T(2,128)S(1)}, f32[1,48,2]{1,2,0:T(2,128)S(1)}, u32[]{:S(2)}, u32[]{:S(2)}) collective-permute-start(f32[1,48,2]{1,2,0:T(2,128)S(1)} %bitcast.260), channel_id=1, source_target_pairs={{0,32},{32,64},{64,96},{1,33},{33,65},{65,97},{2,34},{34,66},{66,9... | collective-permute-start | bytes 1160 | tf_op jit(solution)/shard_map/while/body/eval_jaxpr/ppermute | solution.py:34
  418.2 14.5 %collective-permute-start = (f32[1,48,2]{1,2,0:T(2,128)S(1)}, f32[1,48,2]{1,2,0:T(2,128)S(1)}, u32[]{:S(2)}, u32[]{:S(2)}) collective-permute-start(f32[1,48,2]{1,2,0:T(2,128)S(1)} %bitcast.260), channel_id=1, source_target_pairs={{0,32},{32,64},{64,96},{1,33},{33,65},{65,97},{2,34},{34,66},{66,9... | collective-permute-start | bytes 1160 | tf_op jit(solution)/shard_map/while/body/eval_jaxpr/ppermute | solution.py:34
  440.9 13.7 %collective-permute-start = (f32[1,48,2]{1,2,0:T(2,128)S(1)}, f32[1,48,2]{1,2,0:T(2,128)S(1)}, u32[]{:S(2)}, u32[]{:S(2)}) collective-permute-start(f32[1,48,2]{1,2,0:T(2,128)S(1)} %bitcast.260), channel_id=1, source_target_pairs={{0,32},{32,64},{64,96},{1,33},{33,65},{65,97},{2,34},{34,66},{66,9... | collective-permute-start | bytes 1160 | tf_op jit(solution)/shard_map/while/body/eval_jaxpr/ppermute | solution.py:34
  462.6 13.7 %collective-permute-start = (f32[1,48,2]{1,2,0:T(2,128)S(1)}, f32[1,48,2]{1,2,0:T(2,128)S(1)}, u32[]{:S(2)}, u32[]{:S(2)}) collective-permute-start(f32[1,48,2]{1,2,0:T(2,128)S(1)} %bitcast.260), channel_id=1, source_target_pairs={{0,32},{32,64},{64,96},{1,33},{33,65},{65,97},{2,34},{34,66},{66,9... | collective-permute-start | bytes 1160 | tf_op jit(solution)/shard_map/while/body/eval_jaxpr/ppermute | solution.py:34
  484.4 13.7 %collective-permute-start = (f32[1,48,2]{1,2,0:T(2,128)S(1)}, f32[1,48,2]{1,2,0:T(2,128)S(1)}, u32[]{:S(2)}, u32[]{:S(2)}) collective-permute-start(f32[1,48,2]{1,2,0:T(2,128)S(1)} %bitcast.260), channel_id=1, source_target_pairs={{0,32},{32,64},{64,96},{1,33},{33,65},{65,97},{2,34},{34,66},{66,9... | collective-permute-start | bytes 1160 | tf_op jit(solution)/shard_map/while/body/eval_jaxpr/ppermute | solution.py:34
  506.2 13.7 %collective-permute-start = (f32[1,48,2]{1,2,0:T(2,128)S(1)}, f32[1,48,2]{1,2,0:T(2,128)S(1)}, u32[]{:S(2)}, u32[]{:S(2)}) collective-permute-start(f32[1,48,2]{1,2,0:T(2,128)S(1)} %bitcast.260), channel_id=1, source_target_pairs={{0,32},{32,64},{64,96},{1,33},{33,65},{65,97},{2,34},{34,66},{66,9... | collective-permute-start | bytes 1160 | tf_op jit(solution)/shard_map/while/body/eval_jaxpr/ppermute | solution.py:34
  528.0 13.7 %collective-permute-start = (f32[1,48,2]{1,2,0:T(2,128)S(1)}, f32[1,48,2]{1,2,0:T(2,128)S(1)}, u32[]{:S(2)}, u32[]{:S(2)}) collective-permute-start(f32[1,48,2]{1,2,0:T(2,128)S(1)} %bitcast.260), channel_id=1, source_target_pairs={{0,32},{32,64},{64,96},{1,33},{33,65},{65,97},{2,34},{34,66},{66,9... | collective-permute-start | bytes 1160 | tf_op jit(solution)/shard_map/while/body/eval_jaxpr/ppermute | solution.py:34
  549.8 13.7 %collective-permute-start = (f32[1,48,2]{1,2,0:T(2,128)S(1)}, f32[1,48,2]{1,2,0:T(2,128)S(1)}, u32[]{:S(2)}, u32[]{:S(2)}) collective-permute-start(f32[1,48,2]{1,2,0:T(2,128)S(1)} %bitcast.260), channel_id=1, source_target_pairs={{0,32},{32,64},{64,96},{1,33},{33,65},{65,97},{2,34},{34,66},{66,9... | collective-permute-start | bytes 1160 | tf_op jit(solution)/shard_map/while/body/eval_jaxpr/ppermute | solution.py:34
  571.6 13.7 %collective-permute-start = (f32[1,48,2]{1,2,0:T(2,128)S(1)}, f32[1,48,2]{1,2,0:T(2,128)S(1)}, u32[]{:S(2)}, u32[]{:S(2)}) collective-permute-start(f32[1,48,2]{1,2,0:T(2,128)S(1)} %bitcast.260), channel_id=1, source_target_pairs={{0,32},{32,64},{64,96},{1,33},{33,65},{65,97},{2,34},{34,66},{66,9... | collective-permute-start | bytes 1160 | tf_op jit(solution)/shard_map/while/body/eval_jaxpr/ppermute | solution.py:34
  593.4 13.7 %collective-permute-start = (f32[1,48,2]{1,2,0:T(2,128)S(1)}, f32[1,48,2]{1,2,0:T(2,128)S(1)}, u32[]{:S(2)}, u32[]{:S(2)}) collective-permute-start(f32[1,48,2]{1,2,0:T(2,128)S(1)} %bitcast.260), channel_id=1, source_target_pairs={{0,32},{32,64},{64,96},{1,33},{33,65},{65,97},{2,34},{34,66},{66,9... | collective-permute-start | bytes 1160 | tf_op jit(solution)/shard_map/while/body/eval_jaxpr/ppermute | solution.py:34
  615.2 13.7 %collective-permute-start = (f32[1,48,2]{1,2,0:T(2,128)S(1)}, f32[1,48,2]{1,2,0:T(2,128)S(1)}, u32[]{:S(2)}, u32[]{:S(2)}) collective-permute-start(f32[1,48,2]{1,2,0:T(2,128)S(1)} %bitcast.260), channel_id=1, source_target_pairs={{0,32},{32,64},{64,96},{1,33},{33,65},{65,97},{2,34},{34,66},{66,9... | collective-permute-start | bytes 1160 | tf_op jit(solution)/shard_map/while/body/eval_jaxpr/ppermute | solution.py:34
  637.0 13.7 %collective-permute-start = (f32[1,48,2]{1,2,0:T(2,128)S(1)}, f32[1,48,2]{1,2,0:T(2,128)S(1)}, u32[]{:S(2)}, u32[]{:S(2)}) collective-permute-start(f32[1,48,2]{1,2,0:T(2,128)S(1)} %bitcast.260), channel_id=1, source_target_pairs={{0,32},{32,64},{64,96},{1,33},{33,65},{65,97},{2,34},{34,66},{66,9... | collective-permute-start | bytes 1160 | tf_op jit(solution)/shard_map/while/body/eval_jaxpr/ppermute | solution.py:34
  658.8 13.7 %collective-permute-start = (f32[1,48,2]{1,2,0:T(2,128)S(1)}, f32[1,48,2]{1,2,0:T(2,128)S(1)}, u32[]{:S(2)}, u32[]{:S(2)}) collective-permute-start(f32[1,48,2]{1,2,0:T(2,128)S(1)} %bitcast.260), channel_id=1, source_target_pairs={{0,32},{32,64},{64,96},{1,33},{33,65},{65,97},{2,34},{34,66},{66,9... | collective-permute-start | bytes 1160 | tf_op jit(solution)/shard_map/while/body/eval_jaxpr/ppermute | solution.py:34
  680.6 13.7 %collective-permute-start = (f32[1,48,2]{1,2,0:T(2,128)S(1)}, f32[1,48,2]{1,2,0:T(2,128)S(1)}, u32[]{:S(2)}, u32[]{:S(2)}) collective-permute-start(f32[1,48,2]{1,2,0:T(2,128)S(1)} %bitcast.260), channel_id=1, source_target_pairs={{0,32},{32,64},{64,96},{1,33},{33,65},{65,97},{2,34},{34,66},{66,9... | collective-permute-start | bytes 1160 | tf_op jit(solution)/shard_map/while/body/eval_jaxpr/ppermute | solution.py:34
  724.1 13.7 %collective-permute-start = (f32[1,48,2]{1,2,0:T(2,128)S(1)}, f32[1,48,2]{1,2,0:T(2,128)S(1)}, u32[]{:S(2)}, u32[]{:S(2)}) collective-permute-start(f32[1,48,2]{1,2,0:T(2,128)S(1)} %bitcast.260), channel_id=1, source_target_pairs={{0,32},{32,64},{64,96},{1,33},{33,65},{65,97},{2,34},{34,66},{66,9... | collective-permute-start | bytes 1160 | tf_op jit(solution)/shard_map/while/body/eval_jaxpr/ppermute | solution.py:34
  789.5 13.7 %collective-permute-start = (f32[1,48,2]{1,2,0:T(2,128)S(1)}, f32[1,48,2]{1,2,0:T(2,128)S(1)}, u32[]{:S(2)}, u32[]{:S(2)}) collective-permute-start(f32[1,48,2]{1,2,0:T(2,128)S(1)} %bitcast.260), channel_id=1, source_target_pairs={{0,32},{32,64},{64,96},{1,33},{33,65},{65,97},{2,34},{34,66},{66,9... | collective-permute-start | bytes 1160 | tf_op jit(solution)/shard_map/while/body/eval_jaxpr/ppermute | solution.py:34
  854.9 13.7 %collective-permute-start = (f32[1,48,2]{1,2,0:T(2,128)S(1)}, f32[1,48,2]{1,2,0:T(2,128)S(1)}, u32[]{:S(2)}, u32[]{:S(2)}) collective-permute-start(f32[1,48,2]{1,2,0:T(2,128)S(1)} %bitcast.260), channel_id=1, source_target_pairs={{0,32},{32,64},{64,96},{1,33},{33,65},{65,97},{2,34},{34,66},{66,9... | collective-permute-start | bytes 1160 | tf_op jit(solution)/shard_map/while/body/eval_jaxpr/ppermute | solution.py:34
  920.3 13.7 %collective-permute-start = (f32[1,48,2]{1,2,0:T(2,128)S(1)}, f32[1,48,2]{1,2,0:T(2,128)S(1)}, u32[]{:S(2)}, u32[]{:S(2)}) collective-permute-start(f32[1,48,2]{1,2,0:T(2,128)S(1)} %bitcast.260), channel_id=1, source_target_pairs={{0,32},{32,64},{64,96},{1,33},{33,65},{65,97},{2,34},{34,66},{66,9... | collective-permute-start | bytes 1160 | tf_op jit(solution)/shard_map/while/body/eval_jaxpr/ppermute | solution.py:34
  985.6 13.7 %collective-permute-start = (f32[1,48,2]{1,2,0:T(2,128)S(1)}, f32[1,48,2]{1,2,0:T(2,128)S(1)}, u32[]{:S(2)}, u32[]{:S(2)}) collective-permute-start(f32[1,48,2]{1,2,0:T(2,128)S(1)} %bitcast.260), channel_id=1, source_target_pairs={{0,32},{32,64},{64,96},{1,33},{33,65},{65,97},{2,34},{34,66},{66,9... | collective-permute-start | bytes 1160 | tf_op jit(solution)/shard_map/while/body/eval_jaxpr/ppermute | solution.py:34
  1007.4 13.7 %collective-permute-start = (f32[1,48,2]{1,2,0:T(2,128)S(1)}, f32[1,48,2]{1,2,0:T(2,128)S(1)}, u32[]{:S(2)}, u32[]{:S(2)}) collective-permute-start(f32[1,48,2]{1,2,0:T(2,128)S(1)} %bitcast.260), channel_id=1, source_target_pairs={{0,32},{32,64},{64,96},{1,33},{33,65},{65,97},{2,34},{34,66},{66,9... | collective-permute-start | bytes 1160 | tf_op jit(solution)/shard_map/while/body/eval_jaxpr/ppermute | solution.py:34
  1051.0 13.7 %collective-permute-start = (f32[1,48,2]{1,2,0:T(2,128)S(1)}, f32[1,48,2]{1,2,0:T(2,128)S(1)}, u32[]{:S(2)}, u32[]{:S(2)}) collective-permute-start(f32[1,48,2]{1,2,0:T(2,128)S(1)} %bitcast.260), channel_id=1, source_target_pairs={{0,32},{32,64},{64,96},{1,33},{33,65},{65,97},{2,34},{34,66},{66,9... | collective-permute-start | bytes 1160 | tf_op jit(solution)/shard_map/while/body/eval_jaxpr/ppermute | solution.py:34
  1072.8 13.7 %collective-permute-start = (f32[1,48,2]{1,2,0:T(2,128)S(1)}, f32[1,48,2]{1,2,0:T(2,128)S(1)}, u32[]{:S(2)}, u32[]{:S(2)}) collective-permute-start(f32[1,48,2]{1,2,0:T(2,128)S(1)} %bitcast.260), channel_id=1, source_target_pairs={{0,32},{32,64},{64,96},{1,33},{33,65},{65,97},{2,34},{34,66},{66,9... | collective-permute-start | bytes 1160 | tf_op jit(solution)/shard_map/while/body/eval_jaxpr/ppermute | solution.py:34
  (80 other events, 886.7 us)
where the time goes:
time: 1110 us; the launch traced here: 1100 us
  starting transfers between devices  413 us (37%)
  waiting for transfers between devices  316 us (28%)
  local copies, waits for them, and re-layouts  158 us (14%)
  other arithmetic  138 us (12%)
  matrix products  64.5 us (6%)
    all_to_all x32, waiting for transfers between devices, relax(): lax.all_to_all(field_out.reshape(regions, capacity, 2), 'region', split_a...  224 us
    ppermute x32, starting transfers between devices, extended(): before = lax.ppermute(last, axis, up)  203 us
    all_to_all x32, starting transfers between devices, relax(): lax.all_to_all(field_out.reshape(regions, capacity, 2), 'region', split_a...  125 us
    all_to_all x1, waiting for transfers between devices, body(): lax.all_to_all(outgoing.reshape(regions, capacity, WIN * WIN), 'region',...  91.2 us
    ppermute x32, starting transfers between devices, extended(): after = lax.ppermute(first, axis, down)  61.5 us
    concatenate x18, other arithmetic, spectra_block(): return jnp.concatenate([spec_real, spec_imag], axis=2).astype(jnp.bfloat16)  59.4 us
    dot_general x18, matrix products, spectra_block(): jnp.einsum('kx,bxj->bkj', left_table, first_segment, preferred_element_ty...  53.2 us
    dynamic_update_slice x18, other arithmetic, spectra_all(): lax.map(lambda members: spectra_block(members, cosine_table, sine_table),...  24.3 us
  transfers between devices with their start and end apart: 100, of which 34 were waited for; matrix products, arithmetic and copies ran while one was open for 15% of the time, Pallas kernels for 0%

commit v1 on v0

v1 whole, which is shorter than its diff:
```python
import functools
import math

import jax
import jax.numpy as jnp
import ml_dtypes
import numpy as np
from jax import lax
from jax.experimental import pallas as pl
from jax.experimental.pallas import tpu as pltpu
from jax.sharding import PartitionSpec as P

WIN = 160
RADIUS = 16
SHIFTS = 33
ITERS = 32
HALF = WIN // 2 + 1
CAP = 3
REGIONS = 32
SECTIONS = 4
WIN_DEV = 48
GROUPS = WIN_DEV // CAP
SHARE = 12
CHUNK = 4
QROWS = 48
TLANES = 40
PHASES = 4
QUARTER = WIN // PHASES

sharpness = 12.0
montage_stiffness = 1.0
section_stiffness = 1.0
anchor_stiffness = 0.05
step_length = 0.2

F32 = jnp.float32
BF16 = jnp.bfloat16
MESH = pl.DeviceIdType.MESH
EMPTY = (1 << 20) + 63


def tables():
    f32 = np.float32
    index = np.arange(WIN)
    step = f32(2.0 * math.pi / WIN)

    def rounded(fn, phase):
        angle = (phase % WIN).astype(f32) * step
        return fn(angle.astype(np.float64)).astype(f32).astype(ml_dtypes.bfloat16).astype(f32)

    phase = index[:, None] * index[None, :]
    cosine, sine = rounded(np.cos, phase), rounded(np.sin, phase)
    back = (np.arange(SHIFTS) - RADIUS)[:, None] * index[None, :]
    back_cos, back_sin = rounded(np.cos, back), rounded(np.sin, back)

    right = np.zeros((PHASES, 256, 256), f32)
    for m in range(PHASES):
        rows = slice(32 * m, 32 * m + WIN)
        right[m, rows, :HALF] = cosine[:, :HALF]
        right[m, rows, 128 : 128 + HALF] = -sine[:, :HALF]
    order = np.concatenate([np.arange(QUARTER) * PHASES + m for m in range(PHASES)])
    c, s = cosine[:, order], sine[:, order]
    left = np.concatenate([np.concatenate([c, s], 1), np.concatenate([-s, c], 1)], 0)
    back_left = np.zeros((2 * QROWS, 2 * WIN), f32)
    back_left[:SHIFTS] = np.concatenate([back_cos, -back_sin], 1)
    back_left[QROWS : QROWS + SHIFTS] = np.concatenate([back_sin, back_cos], 1)
    weight = np.full(HALF, 2.0, f32)
    weight[0] = weight[-1] = 1.0
    back_right = np.zeros((512, 128), f32)
    energy = np.zeros((256, 128), f32)
    member = np.zeros((2, 8, 128), f32)
    for i in range(CAP):
        rows, lanes = HALF * i, TLANES * i
        back_right[rows : rows + HALF, lanes : lanes + SHIFTS] = weight[:, None] * back_cos[:, :HALF].T
        back_right[256 + rows : 256 + rows + HALF, lanes : lanes + SHIFTS] = (
            -weight[:, None] * back_sin[:, :HALF].T
        )
        energy[rows : rows + HALF, lanes : lanes + TLANES] = weight[:, None]
        member[0, i, lanes : lanes + SHIFTS] = 1.0
        member[1, CAP + i, lanes : lanes + SHIFTS] = 1.0
    return [jnp.asarray(t.astype(ml_dtypes.bfloat16)) for t in (right, left, back_left, back_right, energy, member)]


def split3(x):
    high = x.astype(BF16)
    rest = x - high.astype(F32)
    middle = rest.astype(BF16)
    low = (rest - middle.astype(F32)).astype(BF16)
    return high, middle, low


def exact_dot(x, table):
    rows = x.shape[0]
    out = jnp.dot(jnp.concatenate(split3(x), axis=0), table, preferred_element_type=F32)
    return out[:rows] + out[rows : 2 * rows] + out[2 * rows :]


def lane_iota(rows=1):
    return lax.broadcasted_iota(jnp.int32, (rows, 128), 1)


def spectra_kernel(
    win_ref, dev_ref, slot_ref, right_ref, left_ref,
    group_ref, slots_ref, place_ref, pick_ref,
    seg_re, seg_im, out_buf, codes, offsets, group_sem, slot_sem,
):
    me = lax.axis_index("region")
    sec = lax.axis_index("sec")

    def clear(k, _):
        codes[k] = EMPTY
        return 0

    lax.fori_loop(0, CAP * REGIONS, clear, 0)

    def insert(j, _):
        device = dev_ref[j]
        offset = (device - me + REGIONS) % REGIONS
        own = jnp.logical_or(
            offset < REGIONS // 2, jnp.logical_and(offset == REGIONS // 2, me < device)
        )
        new = jnp.where(own, j, slot_ref[j]) * 64 + j
        at = CAP * offset
        a, b, c = codes[at], codes[at + 1], codes[at + 2]
        codes[at] = jnp.minimum(a, new)
        new = jnp.maximum(a, new)
        codes[at + 1] = jnp.minimum(b, new)
        new = jnp.maximum(b, new)
        codes[at + 2] = jnp.minimum(c, new)
        return 0

    lax.fori_loop(0, WIN_DEV, insert, 0)

    def compact(o, count):
        offsets[count] = o
        return count + jnp.where(codes[CAP * o] < EMPTY, 1, 0)

    lax.fori_loop(1, REGIONS, compact, 0)

    for m in range(PHASES):
        for part in range(5):
            rows = [
                win_ref[:, 640 * q + 128 * m : 640 * q + 128 * m + 256]
                for q in range(8 * part, 8 * part + 8)
            ]
            seg = jnp.dot(
                jnp.concatenate(rows, axis=0), right_ref[m], preferred_element_type=F32
            )
            start = (QUARTER * m + 8 * part) * WIN_DEV
            seg_re[start : start + 8 * WIN_DEV, :] = seg[:, :128]
            seg_im[start : start + 8 * WIN_DEV, :] = seg[:, 128:]

    place_ref[...] = jnp.zeros_like(place_ref)
    lane = lane_iota()
    wide = lane_iota(WIN)

    def group(g, picks):
        o = offsets[g]
        members = [codes[CAP * o + i] % 64 for i in range(CAP)]
        sides = []
        for seg in (seg_re, seg_im):
            x0, x1, x2 = [seg[pl.ds(w, WIN, stride=WIN_DEV), :] for w in members]
            x1 = pltpu.roll(x1, HALF, 1)
            x2 = pltpu.roll(x2, 2 * HALF - 128, 1)
            sides.append(
                jnp.concatenate(
                    [jnp.where(wide < HALF, x0, x1), jnp.where(wide < 2 * HALF - 128, x1, x2)],
                    axis=1,
                ).astype(BF16)
            )
        spectrum = jnp.dot(
            left_ref[...], jnp.concatenate(sides, axis=0), preferred_element_type=F32
        )
        out_buf[g] = spectrum.astype(BF16)
        pltpu.make_async_copy(out_buf.at[g], group_ref.at[g], group_sem.at[g]).start()
        pltpu.make_async_copy(out_buf.at[g], slots_ref.at[o], slot_sem.at[g]).start()
        for edge in range(SECTIONS - 1):
            row = (lane == REGIONS * edge + o).astype(F32)
            place_ref[pl.ds(GROUPS * edge + g, 1), :] = row
        valid = jnp.where(lane % REGIONS == o, 1, picks[CAP])
        return tuple(
            jnp.where(lane == w, REGIONS * sec + o, pick) for w, pick in zip(members, picks)
        ) + (valid,)

    start = tuple(jnp.full((1, 128), -1, jnp.int32) for _ in range(CAP))
    picks = lax.fori_loop(0, GROUPS, group, start + (jnp.zeros((1, 128), jnp.int32),))
    pick_ref[...] = jnp.concatenate(picks + picks, axis=0)

    def finish(g, _):
        o = offsets[g]
        pltpu.make_async_copy(out_buf.at[g], group_ref.at[g], group_sem.at[g]).wait()
        pltpu.make_async_copy(out_buf.at[g], slots_ref.at[o], slot_sem.at[g]).wait()
        return 0

    lax.fori_loop(0, GROUPS, finish, 0)


SECTION_RECV = (
    ((1, 0), (1, 1), (1, 2)),
    ((0, 3), (2, 0), (2, 1)),
    ((1, 2), (1, 3), (3, 0)),
    ((2, 1), (2, 2), (2, 3)),
)


def section_sends(section):
    return [
        (to, source, chunk)
        for to in range(SECTIONS)
        for chunk, (origin, source) in enumerate(SECTION_RECV[to])
        if origin == section
    ]


def flow_kernel(
    group_ref, slots_ref, place_ref, back_left_ref, back_right_ref, energy_ref, member_ref,
    out_ref,
    local_groups, local_slots, from_section, from_region, cross, backs, squares, sums, gathered, mine, field, fields,
    local_sem, sec_send, sec_recv, reg_send, reg_recv, p1_send, p1_recv, p2_send, p2_recv,
):
    me = lax.axis_index("region")
    sec = lax.axis_index("sec")
    half = REGIONS // 2

    def neighbour(o):
        return {"region": (me + o) % REGIONS}

    barrier = pltpu.get_barrier_semaphore()

    def greet(o, _):
        pl.semaphore_signal(barrier, inc=1, device_id=neighbour(o), device_id_type=MESH)
        return 0

    lax.fori_loop(1, REGIONS, greet, 0)
    for d in range(1, SECTIONS):
        pl.semaphore_signal(
            barrier, inc=1, device_id={"sec": (sec + d) % SECTIONS}, device_id_type=MESH
        )
    pl.semaphore_wait(barrier, REGIONS - 1 + SECTIONS - 1)

    def section_copy(k, index):
        to, source, chunk = section_sends(k)[index]
        return pltpu.make_async_remote_copy(
            src_ref=group_ref.at[pl.ds(CHUNK * source, CHUNK)],
            dst_ref=from_section.at[pl.ds(CHUNK * chunk, CHUNK)],
            send_sem=sec_send.at[index],
            recv_sem=sec_recv.at[chunk],
            device_id={"sec": to},
            device_id_type=MESH,
        )

    def region_copy(o):
        return pltpu.make_async_remote_copy(
            src_ref=slots_ref.at[o],
            dst_ref=from_region.at[o - 1],
            send_sem=reg_send.at[o - 1],
            recv_sem=reg_recv.at[o - 1],
            device_id=neighbour(o),
            device_id_type=MESH,
        )

    for k in range(SECTIONS):

        @pl.when(sec == k)
        def _():
            for index in range(len(section_sends(k))):
                section_copy(k, index).start()

    def send_region(o, _):
        region_copy(o).start()
        return 0

    lax.fori_loop(1, half + 1, send_region, 0)

    keep_slots = pltpu.make_async_copy(slots_ref.at[pl.ds(half, half)], local_slots, local_sem.at[0])
    keep_groups = pltpu.make_async_copy(group_ref, local_groups, local_sem.at[1])
    keep_slots.start()
    keep_groups.start()
    sums[...] = jnp.zeros_like(sums)
    keep_slots.wait()
    keep_groups.wait()

    lane = lane_iota()
    row_shift = lax.broadcasted_iota(jnp.int32, (QROWS, 128), 0)
    shift_mask = jnp.logical_and(row_shift < SHIFTS, lane_iota(QROWS) % TLANES < SHIFTS)
    row_value = (row_shift - RADIUS).astype(F32)

    def correlate(first_ref, second_ref, u):
        energy_a = jnp.zeros((8, 256), F32)
        energy_b = jnp.zeros((8, 256), F32)
        for r in range(0, WIN, 32):
            ar = first_ref[r : r + 32, :].astype(F32)
            ai = first_ref[WIN + r : WIN + r + 32, :].astype(F32)
            br = second_ref[r : r + 32, :].astype(F32)
            bi = second_ref[WIN + r : WIN + r + 32, :].astype(F32)
            scale = 1.0 / (WIN * WIN)
            cross[u, r : r + 32, :] = ((ar * br + ai * bi) * scale).astype(BF16)
            cross[u, WIN + r : WIN + r + 32, :] = ((ai * br - ar * bi) * scale).astype(BF16)
            energy_a += jnp.sum((ar * ar + ai * ai).reshape(4, 8, 256), axis=0)
            energy_b += jnp.sum((br * br + bi * bi).reshape(4, 8, 256), axis=0)
        squares[16 * u : 16 * u + 8, :] = energy_a
        squares[16 * u + 8 : 16 * u + 16, :] = energy_b
        back = jnp.dot(back_left_ref[...], cross[u], preferred_element_type=F32).astype(BF16)
        backs[QROWS * u : QROWS * u + QROWS, :256] = back[:QROWS]
        backs[QROWS * u : QROWS * u + QROWS, 256:] = back[QROWS:]

    def weigh(rows):
        surfaces = jnp.dot(backs[...], back_right_ref[...], preferred_element_type=F32)
        energies = exact_dot(squares[...], energy_ref[...]) / (WIN * WIN)
        for u, row in enumerate(rows):
            first = jnp.sum(energies[16 * u : 16 * u + 8], axis=0, keepdims=True)
            second = jnp.sum(energies[16 * u + 8 : 16 * u + 16], axis=0, keepdims=True)
            norm = jnp.sqrt(first * second + 1e-06)
            surface = surfaces[QROWS * u : QROWS * u + QROWS]
            weights = jnp.where(shift_mask, jnp.exp(sharpness * (surface / norm)), 0.0)
            sums[0, pl.ds(row, 1), :] = jnp.sum(weights, axis=0, keepdims=True)
            sums[1, pl.ds(row, 1), :] = jnp.sum(weights * row_value, axis=0, keepdims=True)

    def section_batch(chunk, _):
        pltpu.make_async_remote_copy(
            src_ref=group_ref.at[pl.ds(0, CHUNK)],
            dst_ref=from_section.at[pl.ds(CHUNK * chunk, CHUNK)],
            send_sem=sec_send.at[0],
            recv_sem=sec_recv.at[chunk],
            device_id={"sec": (sec + 1) % SECTIONS},
            device_id_type=MESH,
        ).wait_recv()
        start = CHUNK * ((SHARE // CHUNK * sec + chunk) % CHUNK)
        for u in range(CHUNK):
            correlate(local_groups.at[start + u], from_section.at[CHUNK * chunk + u], u)
        weigh([half + CHUNK * chunk + u for u in range(CHUNK)])
        return 0

    lax.fori_loop(0, SHARE // CHUNK, section_batch, 0)

    def region_batch(batch, _):
        for u in range(CHUNK):
            o = CHUNK * batch + u + 1
            region_copy(o).wait_recv()
            correlate(local_slots.at[half - o], from_region.at[o - 1], u)
        weigh([half - (CHUNK * batch + u + 1) for u in range(CHUNK)])
        return 0

    lax.fori_loop(0, half // CHUNK, region_batch, 0)

    nt = (((1,), (1,)), ((), ()))

    def turned(table, x):
        parts = [
            lax.dot_general(table, part, nt, preferred_element_type=F32) for part in split3(x)
        ]
        return parts[0] + parts[1] + parts[2]

    column_value = (lane % TLANES - RADIUS).astype(F32)
    total = turned(member_ref[0] + member_ref[1], sums[0])
    moment = turned(member_ref[0], sums[1]) + turned(member_ref[1], sums[0] * column_value)
    flows = moment / jnp.where(total == 0.0, 1.0, total)
    lane8 = lane_iota(8)
    swapped = jnp.logical_and(lane8 >= half, lane8 < half + CHUNK * sec)
    flows = jnp.where(swapped, -flows, flows)
    mine[...] = flows

    def p1_copy(d):
        return pltpu.make_async_remote_copy(
            src_ref=mine,
            dst_ref=gathered.at[d - 1],
            send_sem=p1_send.at[d - 1],
            recv_sem=p1_recv.at[d - 1],
            device_id={"sec": (sec + d) % SECTIONS},
            device_id_type=MESH,
        )

    for d in range(1, SECTIONS):
        p1_copy(d).start()
    for d in range(1, SECTIONS):
        p1_copy(d).wait_recv()
    montage = jnp.zeros((8, 128), F32)
    section = jnp.zeros((8, 128), F32)
    for k in range(SECTIONS):
        block = flows
        for d in range(1, SECTIONS):
            block = jnp.where((sec - k + SECTIONS) % SECTIONS == d, gathered[d - 1], block)
        moved = pltpu.roll(block, (REGIONS * k + half) % 128, 1)
        here = jnp.logical_and(lane8 >= REGIONS * k + half, lane8 < REGIONS * k + REGIONS)
        montage = jnp.where(here, moved, montage)
        moved = pltpu.roll(block, (SHARE * k - half + 128) % 128, 1)
        here = jnp.logical_and(lane8 >= SHARE * k, lane8 < SHARE * k + SHARE)
        section = jnp.where(here, moved, section)
    section = exact_dot(section, place_ref[...].astype(BF16))
    field[0] = montage
    field[1] = section
    fields[0] = field[...]

    def p2_copy(o):
        return pltpu.make_async_remote_copy(
            src_ref=field,
            dst_ref=fields.at[REGIONS - o],
            send_sem=p2_send.at[o - 1],
            recv_sem=p2_recv.at[REGIONS - 1 - o],
            device_id=neighbour(o),
            device_id_type=MESH,
        )

    def p2_start(o, _):
        p2_copy(o).start()
        return 0

    def p2_wait(o, _):
        p2_copy(o).wait_recv()
        return 0

    lax.fori_loop(1, REGIONS, p2_start, 0)
    lax.fori_loop(1, REGIONS, p2_wait, 0)
    out_ref[...] = fields[...]

    for k in range(SECTIONS):

        @pl.when(sec == k)
        def _():
            for index in range(len(section_sends(k))):
                section_copy(k, index).wait_send()

    def sent_region(o, _):
        region_copy(o).wait_send()
        return 0

    lax.fori_loop(1, half + 1, sent_region, 0)
    for d in range(1, SECTIONS):
        p1_copy(d).wait_send()

    def p2_sent(o, _):
        p2_copy(o).wait_send()
        return 0

    lax.fori_loop(1, REGIONS, p2_sent, 0)


def relax_kernel(fields_ref, pick_ref, montage_ref, section_ref, shift_ref):
    lane8 = lane_iota(8)
    slot = lane8 % REGIONS
    valid = jnp.broadcast_to(pick_ref[CAP : CAP + 1, :], (8, 128)) == 1
    montage = fields_ref[0, 0]
    section = fields_ref[0, 1]
    partner_section = jnp.zeros((8, 128), F32)
    for o in range(1, REGIONS):
        turn = (2 * o - REGIONS) % 128
        here = slot == o
        theirs = fields_ref[o, 1]
        partner_section = jnp.where(here, pltpu.roll(theirs, turn, 1) if turn else theirs, partner_section)
        if o < REGIONS // 2:
            montage = jnp.where(here, -pltpu.roll(fields_ref[o, 0], turn, 1), montage)
    montage = jnp.where(valid, montage, 0.0)
    section = jnp.where(valid, section, 0.0)
    partner_section = jnp.where(valid, partner_section, 0.0)
    has_next = jnp.where(lane8 < REGIONS * (SECTIONS - 1), 1.0, 0.0)
    has_prev = jnp.where(lane8 >= REGIONS, 1.0, 0.0)
    disagreement = 2.0 * montage

    def before(x):
        return pltpu.roll(x, REGIONS, 1)

    def after(x):
        return pltpu.roll(x, 128 - REGIONS, 1)

    def step(u, p, apart, flow, previous):
        gradient = (
            montage_stiffness * (2.0 * u - 2.0 * p - apart)
            + section_stiffness * has_next * (u - after(u) - flow)
            - section_stiffness * has_prev * (before(u) - u - previous)
            + anchor_stiffness * u
        )
        return u - step_length * gradient

    previous, partner_previous = before(section), before(partner_section)

    def turn(_, state):
        u, p = state
        return (
            step(u, p, disagreement, section, previous),
            step(p, u, -disagreement, partner_section, partner_previous),
        )

    zero = jnp.zeros((8, 128), F32)
    shift, _ = lax.fori_loop(0, ITERS, turn, (zero, zero))

    values = jnp.concatenate([montage, section, shift], axis=0)
    row = lax.broadcasted_iota(jnp.int32, (128, 128), 0)
    picked = []
    for i in range(CAP):
        wanted = jnp.broadcast_to(pick_ref[i : i + 1, :], (128, 128))
        picked.append(exact_dot(values, (row == wanted).astype(F32).astype(BF16)))
    for k, ref in enumerate((montage_ref, section_ref, shift_ref)):
        for c in range(2):
            total = sum(picked[i][8 * k + CAP * c + i : 8 * k + CAP * c + i + 1] for i in range(CAP))
            ref[0, c : c + 1, :] = total[:, :WIN_DEV]


VMEM = pl.BlockSpec(memory_space=pltpu.VMEM)
SMEM = pl.BlockSpec(memory_space=pltpu.SMEM)
ANY = pl.BlockSpec(memory_space=pl.ANY)


def body(windows, partner_dev, partner_slot):
    right, left, back_left, back_right, energy, member = tables()
    side = (2 * WIN, 256)
    groups, slots, place, pick = pl.pallas_call(
        spectra_kernel,
        out_shape=(
            jax.ShapeDtypeStruct((GROUPS,) + side, BF16),
            jax.ShapeDtypeStruct((REGIONS,) + side, BF16),
            jax.ShapeDtypeStruct((128, 128), F32),
            jax.ShapeDtypeStruct((8, 128), jnp.int32),
        ),
        in_specs=[VMEM, SMEM, SMEM, VMEM, VMEM],
        out_specs=(ANY, ANY, VMEM, VMEM),
        scratch_shapes=[
            pltpu.VMEM((WIN * WIN_DEV, 128), F32),
            pltpu.VMEM((WIN * WIN_DEV, 128), F32),
            pltpu.VMEM((GROUPS,) + side, BF16),
            pltpu.SMEM((CAP * REGIONS,), jnp.int32),
            pltpu.SMEM((REGIONS,), jnp.int32),
            pltpu.SemaphoreType.DMA((GROUPS,)),
            pltpu.SemaphoreType.DMA((GROUPS,)),
        ],
        compiler_params=pltpu.CompilerParams(vmem_limit_bytes=48 << 20),
        name="spectra",
    )(windows[0], partner_dev, partner_slot, right, left)
    half = REGIONS // 2
    fields = pl.pallas_call(
        flow_kernel,
        out_shape=jax.ShapeDtypeStruct((REGIONS, 2, 8, 128), F32),
        in_specs=[ANY, ANY, VMEM, VMEM, VMEM, VMEM, VMEM],
        out_specs=VMEM,
        scratch_shapes=[
            pltpu.VMEM((GROUPS,) + side, BF16),
            pltpu.VMEM((half,) + side, BF16),
            pltpu.VMEM((SHARE,) + side, BF16),
            pltpu.VMEM((half,) + side, BF16),
            pltpu.VMEM((CHUNK,) + side, BF16),
            pltpu.VMEM((CHUNK * QROWS, 512), BF16),
            pltpu.VMEM((CHUNK * 16, 256), F32),
            pltpu.VMEM((2, 128, 128), F32),
            pltpu.VMEM((SECTIONS - 1, 8, 128), F32),
            pltpu.VMEM((8, 128), F32),
            pltpu.VMEM((2, 8, 128), F32),
            pltpu.VMEM((REGIONS, 2, 8, 128), F32),
            pltpu.SemaphoreType.DMA((2,)),
            pltpu.SemaphoreType.DMA((5,)),
            pltpu.SemaphoreType.DMA((SHARE // CHUNK,)),
            pltpu.SemaphoreType.DMA((half,)),
            pltpu.SemaphoreType.DMA((half,)),
            pltpu.SemaphoreType.DMA((SECTIONS - 1,)),
            pltpu.SemaphoreType.DMA((SECTIONS - 1,)),
            pltpu.SemaphoreType.DMA((REGIONS - 1,)),
            pltpu.SemaphoreType.DMA((REGIONS - 1,)),
        ],
        compiler_params=pltpu.CompilerParams(
            vmem_limit_bytes=48 << 20, collective_id=0, has_side_effects=True
        ),
        name="flows",
    )(groups, slots, place, back_left, back_right, energy, member)
    out = jax.ShapeDtypeStruct((1, 2, WIN_DEV), F32)
    return pl.pallas_call(
        relax_kernel,
        out_shape=(out, out, out),
        in_specs=[VMEM, VMEM],
        out_specs=(VMEM, VMEM, VMEM),
        name="relax",
    )(fields, pick)


def solution(mesh):
    placed = (P("sec", "region", None), P("region"), P("region"))
    return jax.shard_map(
        body,
        mesh=mesh,
        in_specs=placed,
        out_specs=(P("sec", None, "region"),) * 3,
        check_vma=False,
    )
```

time: 1110 us -> 116 us (0.10)
  the two profiles are of different devices: /device:TPU:1 before, /device:TPU:30 now
where the time goes in v1:
time: 116 us
  Pallas kernels  109 us (94%)
  local copies, waits for them, and re-layouts  6.29 us (5%)
    pallas_call x1, Pallas kernels, body(): pl.pallas_call(flow_kernel, out_shape=jax.ShapeDtypeStruct((REGIONS, 2, 8...  88.6 us
    pallas_call x1, Pallas kernels, body(): pl.pallas_call(spectra_kernel, out_shape=(jax.ShapeDtypeStruct((GROUPS,)...  15.8 us
    unnamed x22, local copies, waits for them, and re-layouts  6.29 us
    pallas_call x1, Pallas kernels, body(): pl.pallas_call(relax_kernel, out_shape=(out, out, out), in_specs=[VMEM, V...  4.36 us

profile of v1, /device:TPU:30, one launch (start us, length us, event | category | flops | bytes accessed | tf_op | source)
XLA Modules:
  0.0 115.7 jit_solution(12290070419083092747)
XLA Ops:
  0.6 0.0 copy-start.8
  0.6 0.0 copy-start
  0.7 1.7 %copy-done = bf16[1,48,25600]{2,1,0:T(8,128)(2,1)S(1)} copy-done((bf16[1,48,25600]{2,1,0:T(8,128)(2,1)S(1)}, bf16[1,48,25600]{2,1,0:T(8,128)(2,1)}, u32[]{:S(2)}) %copy-start) | copy-done | bytes 2457624
  2.3 0.0 copy-start.2
  2.3 1.0 copy-done.2
  3.4 0.0 copy-start.3
  3.4 0.9 copy-done.3
  4.3 0.0 copy-start.9
  4.3 0.7 copy-done.9
  5.0 0.0 copy-start.10
  5.0 0.7 copy-done.10
  5.6 0.0 copy-start.4
  5.6 0.0 copy-start.5
  5.6 15.8 %spectra.1 = (bf16[16,320,256]{2,1,0:T(8,128)(2,1)S(1)}, bf16[32,320,256]{2,1,0:T(8,128)(2,1)}, f32[128,128]{1,0:T(8,128)S(1)}, s32[8,128]{1,0:T(8,128)S(1)}) custom-call(bf16[48,25600]{1,0:T(8,128)(2,1)S(1)} %bitcast.1, s32[48]{0:T(128)S(1)} %copy-done.9, s32[48]{0:T(128)S(1)} %copy-done.10, bf16[4,256,256]{2,1,0:T(8,128)(2,1)S(1)} %copy-done.2, ...), custom_call_target="tpu_custom_call" | custom-call | tf_op jit(solution)/shard_map/spectra/pallas_call | solution.py:506
  21.4 0.0 copy-start.7
  21.4 0.6 copy-done.7
  22.0 0.0 copy-done.8
  22.0 0.0 copy-done.4
  22.0 0.0 copy-done.5
  22.0 0.0 copy-done.6
  22.0 88.6 %flows.1.fields_ref = f32[32,2,8,128]{3,2,1,0:T(8,128)S(1)} custom-call(bf16[16,320,256]{2,1,0:T(8,128)(2,1)S(1)} %get-tuple-element.7.group_ref, bf16[32,320,256]{2,1,0:T(8,128)(2,1)} %get-tuple-element.8.slots_ref, f32[128,128]{1,0:T(8,128)S(1)} %get-tuple-element.9.place_ref, bf16[96,320]{1,0:T(8,128)(2,1)S(1)} %copy-done.5, ...), custom_call_target="tpu_custom_call" | custom-call | tf_op jit(solution)/shard_map/flows/pallas_call | solution.py:529
  110.6 0.0 copy-start.1
  110.6 0.7 copy-done.1
  111.3 4.4 %relax.1 = (f32[1,2,48]{2,1,0:T(2,128)}, f32[1,2,48]{2,1,0:T(2,128)}, f32[1,2,48]{2,1,0:T(2,128)}) custom-call(f32[32,2,8,128]{3,2,1,0:T(8,128)} %copy-done.1, s32[8,128]{1,0:T(8,128)} %copy-done.7), custom_call_target="tpu_custom_call" | custom-call | tf_op jit(solution)/shard_map/relax/pallas_call | solution.py:563
  (1 shorter events, 0.0 us)
Async XLA Ops:
  0.6 21.4 %copy-start.8 = (bf16[2,8,128]{2,1,0:T(8,128)(2,1)S(1)}, bf16[2,8,128]{2,1,0:T(8,128)(2,1)}, u32[]{:S(2)}) copy-start(bf16[2,8,128]{2,1,0:T(8,128)(2,1)} %constant.17.clone.member_ref) | copy-start | bytes 12292
  0.6 1.7 %copy-start = (bf16[1,48,25600]{2,1,0:T(8,128)(2,1)S(1)}, bf16[1,48,25600]{2,1,0:T(8,128)(2,1)}, u32[]{:S(2)}) copy-start(bf16[1,48,25600]{2,1,0:T(8,128)(2,1)} %param.9) | copy-start | bytes 7372804
  2.3 1.0 copy-start.2
  3.4 0.9 copy-start.3
  4.3 0.7 copy-start.9
  5.0 0.7 copy-start.10
  5.6 16.4 %copy-start.4 = (bf16[512,128]{1,0:T(8,128)(2,1)S(1)}, bf16[512,128]{1,0:T(8,128)(2,1)}, u32[]{:S(2)}) copy-start(bf16[512,128]{1,0:T(8,128)(2,1)} %constant.15.clone.back_right_ref) | copy-start | bytes 393220
  5.6 16.4 %copy-start.5 = (bf16[96,320]{1,0:T(8,128)(2,1)S(1)}, bf16[96,320]{1,0:T(8,128)(2,1)}, u32[]{:S(2)}) copy-start(bf16[96,320]{1,0:T(8,128)(2,1)} %constant.14.clone.back_left_ref) | copy-start | bytes 184324
  5.6 16.4 %copy-start.6 = (bf16[256,128]{1,0:T(8,128)(2,1)S(1)}, bf16[256,128]{1,0:T(8,128)(2,1)}, u32[]{:S(2)}) copy-start(bf16[256,128]{1,0:T(8,128)(2,1)} %constant.16.clone.energy_ref) | copy-start | bytes 196612
  21.4 0.6 copy-start.7
  110.6 0.7 copy-start.1

commit v2 on v1

v2 whole, which is shorter than its diff:
```python
import functools
import math

import jax
import jax.numpy as jnp
import ml_dtypes
import numpy as np
from jax import lax
from jax.experimental import pallas as pl
from jax.experimental.pallas import tpu as pltpu
from jax.sharding import PartitionSpec as P

WIN = 160
RADIUS = 16
SHIFTS = 33
ITERS = 32
HALF = WIN // 2 + 1
CAP = 3
REGIONS = 32
SECTIONS = 4
WIN_DEV = 48
GROUPS = WIN_DEV // CAP
SHARE = 12
CHUNK = 4
QROWS = 48
TLANES = 40
PHASES = 4
QUARTER = WIN // PHASES
PARTS = 5
STEPS_DEV = REGIONS // 2
QUARTERS = GROUPS // CHUNK

sharpness = 12.0
montage_stiffness = 1.0
section_stiffness = 1.0
anchor_stiffness = 0.05
step_length = 0.2

F32 = jnp.float32
BF16 = jnp.bfloat16
MESH = pl.DeviceIdType.MESH
EMPTY = 1 << 20


def tables():
    f32 = np.float32
    index = np.arange(WIN)
    step = f32(2.0 * math.pi / WIN)

    def rounded(fn, phase):
        angle = (phase % WIN).astype(f32) * step
        return fn(angle.astype(np.float64)).astype(f32).astype(ml_dtypes.bfloat16).astype(f32)

    phase = index[:, None] * index[None, :]
    cosine, sine = rounded(np.cos, phase), rounded(np.sin, phase)
    back = (np.arange(SHIFTS) - RADIUS)[:, None] * index[None, :]
    back_cos, back_sin = rounded(np.cos, back), rounded(np.sin, back)

    right = np.zeros((PHASES, 256, 256), f32)
    for m in range(PHASES):
        rows = slice(32 * m, 32 * m + WIN)
        right[m, rows, :HALF] = cosine[:, :HALF]
        right[m, rows, 128 : 128 + HALF] = -sine[:, :HALF]
    order = np.concatenate([np.arange(QUARTER) * PHASES + m for m in range(PHASES)])
    c, s = cosine[:, order], sine[:, order]
    left = np.concatenate([np.concatenate([c, s], 1), np.concatenate([-s, c], 1)], 0)
    back_left = np.zeros((2 * QROWS, 2 * WIN), f32)
    back_left[:SHIFTS] = np.concatenate([back_cos, -back_sin], 1)
    back_left[QROWS : QROWS + SHIFTS] = np.concatenate([back_sin, back_cos], 1)
    weight = np.full(HALF, 2.0, f32)
    weight[0] = weight[-1] = 1.0
    back_right = np.zeros((512, 128), f32)
    energy = np.zeros((256, 128), f32)
    member = np.zeros((2, 8, 128), f32)
    for i in range(CAP):
        rows, lanes = HALF * i, TLANES * i
        back_right[rows : rows + HALF, lanes : lanes + SHIFTS] = weight[:, None] * back_cos[:, :HALF].T
        back_right[256 + rows : 256 + rows + HALF, lanes : lanes + SHIFTS] = (
            -weight[:, None] * back_sin[:, :HALF].T
        )
        energy[rows : rows + HALF, lanes : lanes + TLANES] = weight[:, None]
        member[0, i, lanes : lanes + SHIFTS] = 1.0
        member[1, CAP + i, lanes : lanes + SHIFTS] = 1.0
    return [jnp.asarray(t.astype(ml_dtypes.bfloat16)) for t in (right, left, back_left, back_right, energy, member)]


def split3(x):
    high = x.astype(BF16)
    rest = x - high.astype(F32)
    middle = rest.astype(BF16)
    low = (rest - middle.astype(F32)).astype(BF16)
    return high, middle, low


def exact_dot(x, table):
    rows = x.shape[0]
    out = jnp.dot(jnp.concatenate(split3(x), axis=0), table, preferred_element_type=F32)
    return out[:rows] + out[rows : 2 * rows] + out[2 * rows :]


def lane_iota(rows=1):
    return lax.broadcasted_iota(jnp.int32, (rows, 128), 1)


SECTION_RECV = (
    ((1, 0), (1, 1), (1, 2)),
    ((0, 3), (2, 0), (2, 1)),
    ((1, 2), (1, 3), (3, 0)),
    ((2, 1), (2, 2), (2, 3)),
)


STEPS = (
    (1, 0, 0), (1, 0, 1), (-1, 0, 1), (1, 0, 2), (0, 0, 1), (2, 0, -1), "y", (0, 0, 2),
    (-1, 1, 0), (-1, 1, -1), (1, 1, -1), (-1, 1, 2), (0, 1, -1), (2, 1, 1), "x", "xz",
)


def moved(me, step, sign):
    y, x, z = me // 8, me // 4 % 2, me % 4
    move = STEPS[step]
    if move == "y":
        upper = y // 2
        move = (2, 0, 2 * (1 - upper) if sign > 0 else 2 * upper)
    elif isinstance(move, str):
        move = (2 * (1 - x) if sign > 0 else 2 * x, 1, 2 if move == "xz" else 0)
    dy, dx, dz = move
    return (y + sign * dy + 4) % 4 * 8 + (x + dx) % 2 * 4 + (z + sign * dz + 4) % 4


def section_sends(section):
    return [
        (to, source, chunk)
        for to in range(SECTIONS)
        for chunk, (origin, source) in enumerate(SECTION_RECV[to])
        if origin == section
    ]


def flow_kernel(
    win_hbm, dev_ref, slot_ref,
    right_hbm, left_hbm, back_left_hbm, back_right_hbm, energy_hbm, member_hbm,
    out_ref,
    right_ref, left_ref, back_left_ref, back_right_ref, energy_ref, member_ref,
    win_ref, seg_re, seg_im, spectra, natural, outgoing, packed, from_section, from_region,
    cross, backs, squares, sums, dev_row, slot_row, ids_vmem, ids, local_ids,
    from_slot, from_group, from_partner, gathered, mine, field, fields,
    load_sem, ids_sem, sec_send, sec_recv, reg_send, reg_recv, p1_send, p1_recv, p2_send, p2_recv,
):
    me = lax.axis_index("region")
    sec = lax.axis_index("sec")

    def neighbour(o):
        return {"region": (me + o) % REGIONS}

    width = WIN * WIN // PARTS
    load_right = pltpu.make_async_copy(right_hbm, right_ref, load_sem.at[PARTS])
    load_tables = [
        pltpu.make_async_copy(source, into, load_sem.at[PARTS + 1 + k])
        for k, (source, into) in enumerate(
            (
                (left_hbm, left_ref),
                (back_left_hbm, back_left_ref),
                (back_right_hbm, back_right_ref),
                (energy_hbm, energy_ref),
                (member_hbm, member_ref),
            )
        )
    ]

    def load_part(part):
        lanes = pl.ds(part * width, width)
        return pltpu.make_async_copy(
            win_hbm.at[0, :, lanes], win_ref.at[:, lanes], load_sem.at[part]
        )

    load_right.start()
    for part in range(PARTS):
        load_part(part).start()
    for load in load_tables:
        load.start()

    barrier = pltpu.get_barrier_semaphore()

    def greet(o, _):
        pl.semaphore_signal(barrier, inc=1, device_id=neighbour(o), device_id_type=MESH)
        return 0

    lax.fori_loop(1, REGIONS, greet, 0)
    for d in range(1, SECTIONS):
        pl.semaphore_signal(
            barrier, inc=1, device_id={"sec": (sec + d) % SECTIONS}, device_id_type=MESH
        )

    lane = lane_iota()
    dev_row[...] = jnp.full((1, 128), -1, jnp.int32)
    slot_row[...] = jnp.full((1, 128), -1, jnp.int32)
    dev_row[0:1, 0:WIN_DEV] = dev_ref[...].reshape(1, WIN_DEV)
    slot_row[0:1, 0:WIN_DEV] = slot_ref[...].reshape(1, WIN_DEV)
    device, partner = dev_row[...], slot_row[...]
    code = jnp.where(me < device, lane, partner) * 64 + lane
    same = device == lax.broadcasted_iota(jnp.int32, (REGIONS, 128), 0)
    left_over = jnp.where(same, code, EMPTY)
    rank = jnp.zeros((1, 128), jnp.int32)
    listed = jnp.zeros((REGIONS, 128), jnp.int32)
    lane32 = lane_iota(REGIONS)
    for i in range(CAP):
        least = jnp.min(left_over, axis=1, keepdims=True)
        found = jnp.logical_and(same, left_over == least)
        rank += i * jnp.sum(jnp.where(found, 1, 0), axis=0, keepdims=True)
        window = jnp.where(least < EMPTY, least % 64, 0)
        listed = jnp.where(lane32 == i, window, listed)
        left_over = jnp.where(left_over > least, left_over, EMPTY)
    ids_vmem[...] = listed
    load_ids = pltpu.make_async_copy(ids_vmem, ids, ids_sem)
    load_ids.start()

    load_right.wait()
    for part in range(PARTS):
        load_part(part).wait()
        for m in range(PHASES):
            rows = [
                win_ref[:, 640 * q + 128 * m : 640 * q + 128 * m + 256]
                for q in range(8 * part, 8 * part + 8)
            ]
            seg = jnp.dot(
                jnp.concatenate(rows, axis=0), right_ref[m], preferred_element_type=F32
            )
            start = (QUARTER * m + 8 * part) * WIN_DEV
            seg_re[start : start + 8 * WIN_DEV, :] = seg[:, :128]
            seg_im[start : start + 8 * WIN_DEV, :] = seg[:, 128:]
    for load in load_tables:
        load.wait()
    load_ids.wait()
    for step in range(STEPS_DEV):
        origin = moved(me, step, -1)
        for i in range(CAP):
            local_ids[CAP * step + i] = ids[origin, i]

    wide = lane_iota(2 * WIN)

    def pack(windows):
        x0, x1, x2 = [spectra[w] for w in windows]
        x1 = pltpu.roll(x1, HALF, 1)
        x2 = pltpu.roll(x2, 2 * HALF - 128, 1)
        return jnp.concatenate(
            [jnp.where(wide < HALF, x0, x1), jnp.where(wide < 2 * HALF - 128, x1, x2)], axis=1
        )

    def section_copy(k, index):
        to, source, chunk = section_sends(k)[index]
        return pltpu.make_async_remote_copy(
            src_ref=natural.at[pl.ds(CHUNK * source, CHUNK)],
            dst_ref=from_section.at[pl.ds(CHUNK * chunk, CHUNK)],
            send_sem=sec_send.at[index],
            recv_sem=sec_recv.at[chunk],
            device_id={"sec": to},
            device_id_type=MESH,
        )

    def region_copy(step):
        to = moved(me, step, 1)
        return pltpu.make_async_remote_copy(
            src_ref=outgoing.at[step],
            dst_ref=from_region.at[step],
            send_sem=reg_send.at[step],
            recv_sem=reg_recv.at[step],
            device_id={"region": to},
            device_id_type=MESH,
        )

    def spectra_step(step, first):
        part = (2 * first + step) % (2 * QUARTERS)
        for pair in range(CAP):
            w = 2 * CAP * part + 2 * pair
            sides = [
                jnp.concatenate(
                    [seg[pl.ds(w + k, WIN, stride=WIN_DEV), :] for k in range(2)], axis=1
                ).astype(BF16)
                for seg in (seg_re, seg_im)
            ]
            spectrum = jnp.dot(
                left_ref[...], jnp.concatenate(sides, axis=0), preferred_element_type=F32
            ).astype(BF16)
            spectra[w] = spectrum[:, :128]
            spectra[w + 1] = spectrum[:, 128:]
        for k in range(2):
            w = 2 * CAP * part + CAP * k
            natural[2 * part + k] = pack([w, w + 1, w + 2])
        return first

    start = jnp.where(sec == 1, 2, 0)
    for quarter in range(QUARTERS):
        lax.fori_loop(2 * quarter, 2 * quarter + 2, spectra_step, start)
        if quarter == 0:
            pl.semaphore_wait(barrier, REGIONS - 1 + SECTIONS - 1)
        for k in range(SECTIONS):
            done = (quarter + (2 if k == 1 else 0)) % QUARTERS

            @pl.when(sec == k)
            def _():
                for index, (_, source, _) in enumerate(section_sends(k)):
                    if source == done:
                        section_copy(k, index).start()

    for step in list(range(STEPS_DEV // 2, STEPS_DEV)) + list(range(STEPS_DEV // 2)):
        to = moved(me, step, 1)
        outgoing[step] = pack([ids[to, i] for i in range(CAP)])
        region_copy(step).start()

    row = lax.broadcasted_iota(jnp.int32, (128, 128), 0)
    column = lax.broadcasted_iota(jnp.int32, (128, 128), 1)
    origin = jnp.full((128, 128), -2, jnp.int32)
    local = jnp.zeros((8, 128), jnp.bool_)
    for step in range(STEPS_DEV):
        origin = jnp.where(row == step, moved(me, step, -1), origin)
        local = jnp.logical_or(local, jnp.broadcast_to(device, (8, 128)) == moved(me, step, -1))
    for i in range(CAP):
        chosen = jnp.logical_and(origin == device, rank == i)
        from_slot[:, 128 * i : 128 * i + 128] = chosen.astype(F32).astype(BF16)
        chosen = CAP * row + i == column
        chosen = jnp.logical_and(chosen, column < WIN_DEV)
        from_group[:, 128 * i : 128 * i + 128] = chosen.astype(F32).astype(BF16)
    from_partner[...] = (row == partner).astype(F32).astype(BF16)

    sums[...] = jnp.zeros_like(sums)
    row_shift = lax.broadcasted_iota(jnp.int32, (QROWS, 128), 0)
    shift_mask = jnp.logical_and(row_shift < SHIFTS, lane_iota(QROWS) % TLANES < SHIFTS)
    row_value = (row_shift - RADIUS).astype(F32)

    def correlate(first_ref, second_ref, u):
        energy_a = jnp.zeros((8, 256), F32)
        energy_b = jnp.zeros((8, 256), F32)
        for r in range(0, WIN, 32):
            ar = first_ref[r : r + 32, :].astype(F32)
            ai = first_ref[WIN + r : WIN + r + 32, :].astype(F32)
            br = second_ref[r : r + 32, :].astype(F32)
            bi = second_ref[WIN + r : WIN + r + 32, :].astype(F32)
            scale = 1.0 / (WIN * WIN)
            cross[u, r : r + 32, :] = ((ar * br + ai * bi) * scale).astype(BF16)
            cross[u, WIN + r : WIN + r + 32, :] = ((ai * br - ar * bi) * scale).astype(BF16)
            energy_a += jnp.sum((ar * ar + ai * ai).reshape(4, 8, 256), axis=0)
            energy_b += jnp.sum((br * br + bi * bi).reshape(4, 8, 256), axis=0)
        squares[16 * u : 16 * u + 8, :] = energy_a
        squares[16 * u + 8 : 16 * u + 16, :] = energy_b
        back = jnp.dot(back_left_ref[...], cross[u], preferred_element_type=F32).astype(BF16)
        backs[QROWS * u : QROWS * u + QROWS, :256] = back[:QROWS]
        backs[QROWS * u : QROWS * u + QROWS, 256:] = back[QROWS:]

    def weigh(rows):
        surfaces = jnp.dot(backs[...], back_right_ref[...], preferred_element_type=F32)
        energies = exact_dot(squares[...], energy_ref[...]) / (WIN * WIN)
        for u, row in enumerate(rows):
            first = jnp.sum(energies[16 * u : 16 * u + 8], axis=0, keepdims=True)
            second = jnp.sum(energies[16 * u + 8 : 16 * u + 16], axis=0, keepdims=True)
            norm = jnp.sqrt(first * second + 1e-06)
            surface = surfaces[QROWS * u : QROWS * u + QROWS]
            weights = jnp.where(shift_mask, jnp.exp(sharpness * (surface / norm)), 0.0)
            sums[0, pl.ds(row, 1), :] = jnp.sum(weights, axis=0, keepdims=True)
            sums[1, pl.ds(row, 1), :] = jnp.sum(weights * row_value, axis=0, keepdims=True)

    def section_batch(chunk, _):
        pltpu.make_async_remote_copy(
            src_ref=natural.at[pl.ds(0, CHUNK)],
            dst_ref=from_section.at[pl.ds(CHUNK * chunk, CHUNK)],
            send_sem=sec_send.at[0],
            recv_sem=sec_recv.at[chunk],
            device_id={"sec": (sec + 1) % SECTIONS},
            device_id_type=MESH,
        ).wait_recv()
        first = CHUNK * ((SHARE // CHUNK * sec + chunk) % QUARTERS)
        for u in range(CHUNK):
            correlate(natural.at[first + u], from_section.at[CHUNK * chunk + u], u)
        weigh([STEPS_DEV + CHUNK * chunk + u for u in range(CHUNK)])
        return 0

    def region_batch(batch, _):
        for u in range(CHUNK):
            step = CHUNK * batch + u
            packed[u] = pack([local_ids[CAP * step + i] for i in range(CAP)])
            pltpu.make_async_remote_copy(
                src_ref=outgoing.at[0],
                dst_ref=from_region.at[step],
                send_sem=reg_send.at[step],
                recv_sem=reg_recv.at[step],
                device_id=neighbour(1),
                device_id_type=MESH,
            ).wait_recv()
            correlate(packed.at[u], from_region.at[step], u)
        weigh([CHUNK * batch + u for u in range(CHUNK)])
        return 0

    batches = STEPS_DEV // CHUNK
    lax.fori_loop(0, batches // 2, region_batch, 0)
    lax.fori_loop(0, SHARE // CHUNK, section_batch, 0)
    lax.fori_loop(batches // 2, batches, region_batch, 0)

    nt = (((1,), (1,)), ((), ()))

    def turned(table, x):
        parts = [
            lax.dot_general(table, part, nt, preferred_element_type=F32) for part in split3(x)
        ]
        return parts[0] + parts[1] + parts[2]

    column_value = (lane % TLANES - RADIUS).astype(F32)
    total = turned(member_ref[0] + member_ref[1], sums[0])
    moment = turned(member_ref[0], sums[1]) + turned(member_ref[1], sums[0] * column_value)
    flows = moment / jnp.where(total == 0.0, 1.0, total)
    lane8 = lane_iota(8)
    swapped = jnp.logical_and(lane8 >= STEPS_DEV, lane8 < STEPS_DEV + CHUNK * sec)
    flows = jnp.where(swapped, -flows, flows)
    flows = jnp.where(jnp.abs(flows) <= 2.0 * RADIUS, flows, 0.0)
    mine[...] = flows

    def p1_copy(d):
        return pltpu.make_async_remote_copy(
            src_ref=mine,
            dst_ref=gathered.at[d - 1],
            send_sem=p1_send.at[d - 1],
            recv_sem=p1_recv.at[d - 1],
            device_id={"sec": (sec + d) % SECTIONS},
            device_id_type=MESH,
        )

    for d in range(1, SECTIONS):
        p1_copy(d).start()
    for d in range(1, SECTIONS):
        p1_copy(d).wait_recv()
    blocks = []
    section = jnp.zeros((8, 128), F32)
    for k in range(SECTIONS):
        block = flows
        for d in range(1, SECTIONS):
            block = jnp.where((sec - k + SECTIONS) % SECTIONS == d, gathered[d - 1], block)
        blocks.append(block)
        turned_block = pltpu.roll(block, (SHARE * k - STEPS_DEV + 128) % 128, 1)
        here = jnp.logical_and(lane8 >= SHARE * k, lane8 < SHARE * k + SHARE)
        section = jnp.where(here, turned_block, section)

    def by_window(x, table):
        spread = exact_dot(x, table)
        rows = []
        for k in range(x.shape[0] // 8):
            for c in range(2):
                at = 8 * k + CAP * c
                rows.append(
                    sum(spread[at + i : at + i + 1, 128 * i : 128 * i + 128] for i in range(CAP))
                )
        return rows

    edges = [section] + [
        pltpu.roll(section, 128 - GROUPS * e, 1) for e in range(1, SECTIONS - 1)
    ]
    edges = [jnp.where(lane8 < GROUPS, edge, 0.0) for edge in edges]
    blocks = [jnp.where(lane8 < STEPS_DEV, block, 0.0) for block in blocks]
    montage_rows = by_window(jnp.concatenate(blocks, axis=0), from_slot[...])
    section_rows = by_window(jnp.concatenate(edges, axis=0), from_group[...])
    montage = jnp.concatenate(montage_rows, axis=0)
    section = jnp.concatenate(section_rows + [jnp.zeros((2, 128), F32)], axis=0)
    field[0:8, :] = montage
    field[8:16, :] = section

    def p2_copy(o):
        return pltpu.make_async_remote_copy(
            src_ref=field,
            dst_ref=fields.at[REGIONS - o],
            send_sem=p2_send.at[o - 1],
            recv_sem=p2_recv.at[REGIONS - 1 - o],
            device_id=neighbour(o),
            device_id_type=MESH,
        )

    def p2_start(o, _):
        p2_copy(o).start()
        return 0

    def p2_wait(o, _):
        p2_copy(o).wait_recv()
        return 0

    lax.fori_loop(1, REGIONS, p2_start, 0)
    lax.fori_loop(1, REGIONS, p2_wait, 0)

    theirs = exact_dot(fields[1:].reshape(16 * (REGIONS - 1), 128), from_partner[...])
    partner_field = jnp.zeros((16, 128), F32)
    for o in range(1, REGIONS):
        here = jnp.broadcast_to(device, (16, 128)) == (me + o) % REGIONS
        partner_field = jnp.where(here, theirs[16 * o - 16 : 16 * o], partner_field)
    montage = jnp.where(local, montage, -partner_field[:8])
    partner_section = partner_field[8:]

    row8 = lax.broadcasted_iota(jnp.int32, (8, 128), 0)
    has_next = jnp.where(row8 < 2 * (SECTIONS - 1), 1.0, 0.0)
    has_prev = jnp.where(row8 >= 2, 1.0, 0.0)
    disagreement = 2.0 * montage

    def before(x):
        return pltpu.roll(x, 2, 0)

    def after(x):
        return pltpu.roll(x, 6, 0)

    def relax(u, p, apart, flow, previous):
        gradient = (
            montage_stiffness * (2.0 * u - 2.0 * p - apart)
            + section_stiffness * has_next * (u - after(u) - flow)
            - section_stiffness * has_prev * (before(u) - u - previous)
            + anchor_stiffness * u
        )
        return u - step_length * gradient

    previous, partner_previous = before(section), before(partner_section)

    def turn(_, state):
        u, p = state
        return (
            relax(u, p, disagreement, section, previous),
            relax(p, u, -disagreement, partner_section, partner_previous),
        )

    zero = jnp.zeros((8, 128), F32)
    shift, _ = lax.fori_loop(0, ITERS, turn, (zero, zero))
    for k, values in enumerate((montage, section, shift)):
        chosen = values[0:2]
        for n in range(1, SECTIONS):
            chosen = jnp.where(sec == n, values[2 * n : 2 * n + 2], chosen)
        out_ref[2 * k : 2 * k + 2, :] = chosen
    out_ref[6:8, :] = jnp.zeros((2, 128), F32)

    for k in range(SECTIONS):

        @pl.when(sec == k)
        def _():
            for index in range(len(section_sends(k))):
                section_copy(k, index).wait_send()

    for step in range(STEPS_DEV):
        region_copy(step).wait_send()
    for d in range(1, SECTIONS):
        p1_copy(d).wait_send()

    def p2_sent(o, _):
        p2_copy(o).wait_send()
        return 0

    lax.fori_loop(1, REGIONS, p2_sent, 0)


def split_kernel(rows_ref, montage_ref, section_ref, shift_ref):
    for k, ref in enumerate((montage_ref, section_ref, shift_ref)):
        ref[0] = rows_ref[2 * k : 2 * k + 2, :WIN_DEV]


VMEM = pl.BlockSpec(memory_space=pltpu.VMEM)
ANY = pl.BlockSpec(memory_space=pl.ANY)


def body(windows, partner_dev, partner_slot):
    side = (2 * WIN, 256)
    dma = pltpu.SemaphoreType.DMA
    rows = pl.pallas_call(
        flow_kernel,
        out_shape=jax.ShapeDtypeStruct((8, 128), F32),
        in_specs=[ANY, VMEM, VMEM] + [ANY] * 6,
        out_specs=VMEM,
        scratch_shapes=[
            pltpu.VMEM((PHASES, 256, 256), BF16),
            pltpu.VMEM((2 * WIN, 2 * WIN), BF16),
            pltpu.VMEM((2 * QROWS, 2 * WIN), BF16),
            pltpu.VMEM((512, 128), BF16),
            pltpu.VMEM((256, 128), BF16),
            pltpu.VMEM((2, 8, 128), BF16),
            pltpu.VMEM((WIN_DEV, WIN * WIN), BF16),
            pltpu.VMEM((WIN * WIN_DEV, 128), F32),
            pltpu.VMEM((WIN * WIN_DEV, 128), F32),
            pltpu.VMEM((WIN_DEV, 2 * WIN, 128), BF16),
            pltpu.VMEM((GROUPS,) + side, BF16),
            pltpu.VMEM((STEPS_DEV,) + side, BF16),
            pltpu.VMEM((CHUNK,) + side, BF16),
            pltpu.VMEM((SHARE,) + side, BF16),
            pltpu.VMEM((STEPS_DEV,) + side, BF16),
            pltpu.VMEM((CHUNK,) + side, BF16),
            pltpu.VMEM((CHUNK * QROWS, 512), BF16),
            pltpu.VMEM((CHUNK * 16, 256), F32),
            pltpu.VMEM((2, 128, 128), F32),
            pltpu.VMEM((1, 128), jnp.int32),
            pltpu.VMEM((1, 128), jnp.int32),
            pltpu.VMEM((REGIONS, 128), jnp.int32),
            pltpu.SMEM((REGIONS, 128), jnp.int32),
            pltpu.SMEM((CAP * STEPS_DEV,), jnp.int32),
            pltpu.VMEM((128, CAP * 128), BF16),
            pltpu.VMEM((128, CAP * 128), BF16),
            pltpu.VMEM((128, 128), BF16),
            pltpu.VMEM((SECTIONS - 1, 8, 128), F32),
            pltpu.VMEM((8, 128), F32),
            pltpu.VMEM((16, 128), F32),
            pltpu.VMEM((REGIONS, 16, 128), F32),
            dma((PARTS + 6,)),
            dma,
            dma((5,)),
            dma((SHARE // CHUNK,)),
            dma((STEPS_DEV,)),
            dma((STEPS_DEV,)),
            dma((SECTIONS - 1,)),
            dma((SECTIONS - 1,)),
            dma((REGIONS - 1,)),
            dma((REGIONS - 1,)),
        ],
        compiler_params=pltpu.CompilerParams(
            vmem_limit_bytes=60 << 20, collective_id=0, has_side_effects=True
        ),
        name="flows",
    )(windows, partner_dev, partner_slot, *tables())
    out = jax.ShapeDtypeStruct((1, 2, WIN_DEV), F32)
    return pl.pallas_call(
        split_kernel,
        out_shape=(out, out, out),
        in_specs=[VMEM],
        out_specs=(VMEM, VMEM, VMEM),
        name="split",
    )(rows)


def solution(mesh):
    placed = (P("sec", "region", None), P("region"), P("region"))
    return jax.shard_map(
        body,
        mesh=mesh,
        in_specs=placed,
        out_specs=(P("sec", None, "region"),) * 3,
        check_vma=False,
    )
```

time: 116 us -> 73.3 us (0.63)
  the two profiles are of different devices: /device:TPU:30 before, /device:TPU:1 now
where the time goes in v2:
time: 73.3 us; the launch traced here: 73.1 us
  Pallas kernels  72.5 us (99%)
    pallas_call x1, Pallas kernels, body(): pl.pallas_call(flow_kernel, out_shape=jax.ShapeDtypeStruct((8, 128), F32)...  71.3 us

profile of v2, /device:TPU:1, one launch (start us, length us, event | category | flops | bytes accessed | tf_op | source)
XLA Modules:
  0.0 73.1 jit_solution(10314217945197691658)
XLA Ops:
  0.6 71.3 %flows.1.rows_ref = f32[8,128]{1,0:T(8,128)} custom-call(bf16[1,48,25600]{2,1,0:T(8,128)(2,1)} %win_hbm.1, s32[48]{0:T(128)} %dev_ref.1, s32[48]{0:T(128)} %slot_ref.1, bf16[4,256,256]{2,1,0:T(8,128)(2,1)} %constant.12.clone.right_hbm, bf16[320,320]{1,0:T(8,128)(2,1)} %constant.13.clone.left_hbm, bf16[96,320]{1,0:T(8,128)(2,1)} %constant.14.clone.back_left_hbm, ...), custom_call_target="tpu_custom_call" | custom-call | tf_op jit(solution)/shard_map/flows/pallas_call | solution.py:562
  71.9 1.3 %split.1 = (f32[1,2,48]{2,1,0:T(2,128)}, f32[1,2,48]{2,1,0:T(2,128)}, f32[1,2,48]{2,1,0:T(2,128)}) custom-call(f32[8,128]{1,0:T(8,128)} %flows.1.rows_ref), custom_call_target="tpu_custom_call" | custom-call | tf_op jit(solution)/shard_map/split/pallas_call | solution.py:616

commit v3 on v2

--- a/solution.py
+++ b/solution.py
@@ -28,6 +28,7 @@
 QUARTER = WIN // PHASES
 PARTS = 5
 STEPS_DEV = REGIONS // 2
+EARLY = STEPS_DEV - CHUNK
 QUARTERS = GROUPS // CHUNK
 
 sharpness = 12.0
@@ -71,7 +72,7 @@
     weight[0] = weight[-1] = 1.0
     back_right = np.zeros((512, 128), f32)
     energy = np.zeros((256, 128), f32)
-    member = np.zeros((2, 8, 128), f32)
+    member = np.zeros((8, 128), f32)
     for i in range(CAP):
         rows, lanes = HALF * i, TLANES * i
         back_right[rows : rows + HALF, lanes : lanes + SHIFTS] = weight[:, None] * back_cos[:, :HALF].T
@@ -79,8 +80,8 @@
             -weight[:, None] * back_sin[:, :HALF].T
         )
         energy[rows : rows + HALF, lanes : lanes + TLANES] = weight[:, None]
-        member[0, i, lanes : lanes + SHIFTS] = 1.0
-        member[1, CAP + i, lanes : lanes + SHIFTS] = 1.0
+        member[i::CAP, lanes : lanes + SHIFTS] = 1.0
+    member[2 * CAP :] = 0.0
     return [jnp.asarray(t.astype(ml_dtypes.bfloat16)) for t in (right, left, back_left, back_right, energy, member)]
 
 
@@ -114,6 +115,7 @@
     (1, 0, 0), (1, 0, 1), (-1, 0, 1), (1, 0, 2), (0, 0, 1), (2, 0, -1), "y", (0, 0, 2),
     (-1, 1, 0), (-1, 1, -1), (1, 1, -1), (-1, 1, 2), (0, 1, -1), (2, 1, 1), "x", "xz",
 )
+MUTUAL = STEPS.index((0, 0, 2))
 
 
 def moved(me, step, sign):
@@ -143,15 +145,28 @@
     out_ref,
     right_ref, left_ref, back_left_ref, back_right_ref, energy_ref, member_ref,
     win_ref, seg_re, seg_im, spectra, natural, outgoing, packed, from_section, from_region,
-    cross, backs, squares, sums, dev_row, slot_row, ids_vmem, ids, local_ids,
-    from_slot, from_group, from_partner, gathered, mine, field, fields,
-    load_sem, ids_sem, sec_send, sec_recv, reg_send, reg_recv, p1_send, p1_recv, p2_send, p2_recv,
+    cross, backs, squares, sums, dev_row, slot_row, ids_vmem, ids,
+    from_slot, from_group, from_partner, published, ours, early, late, sections, field, fields,
+    load_sem, ids_sem, sec_send, sec_recv, reg_send, reg_recv,
+    field_send, field_recv, ours_send, ours_recv, early_send, early_recv, late_send, late_recv, ready,
 ):
     me = lax.axis_index("region")
     sec = lax.axis_index("sec")
 
     def neighbour(o):
         return {"region": (me + o) % REGIONS}
+
+    barrier = pltpu.get_barrier_semaphore()
+
+    def greet(o, _):
+        pl.semaphore_signal(barrier, inc=1, device_id=neighbour(o), device_id_type=MESH)
+        return 0
+
+    lax.fori_loop(1, REGIONS, greet, 0)
+    for d in range(1, SECTIONS):
+        pl.semaphore_signal(
+            barrier, inc=1, device_id={"sec": (sec + d) % SECTIONS}, device_id_type=MESH
+        )
 
     width = WIN * WIN // PARTS
     load_right = pltpu.make_async_copy(right_hbm, right_ref, load_sem.at[PARTS])
@@ -179,18 +194,6 @@
         load_part(part).start()
     for load in load_tables:
         load.start()
-
-    barrier = pltpu.get_barrier_semaphore()
-
-    def greet(o, _):
-        pl.semaphore_signal(barrier, inc=1, device_id=neighbour(o), device_id_type=MESH)
-        return 0
-
-    lax.fori_loop(1, REGIONS, greet, 0)
-    for d in range(1, SECTIONS):
-        pl.semaphore_signal(
-            barrier, inc=1, device_id={"sec": (sec + d) % SECTIONS}, device_id_type=MESH
-        )
 
     lane = lane_iota()
     dev_row[...] = jnp.full((1, 128), -1, jnp.int32)
@@ -232,10 +235,6 @@
     for load in load_tables:
         load.wait()
     load_ids.wait()
-    for step in range(STEPS_DEV):
-        origin = moved(me, step, -1)
-        for i in range(CAP):
-            local_ids[CAP * step + i] = ids[origin, i]
 
     wide = lane_iota(2 * WIN)
 
@@ -294,6 +293,10 @@
         lax.fori_loop(2 * quarter, 2 * quarter + 2, spectra_step, start)
         if quarter == 0:
             pl.semaphore_wait(barrier, REGIONS - 1 + SECTIONS - 1)
+            for d in range(1, SECTIONS):
+                pl.semaphore_signal(
+                    ready, inc=1, device_id={"sec": (sec + d) % SECTIONS}, device_id_type=MESH
+                )
         for k in range(SECTIONS):
             done = (quarter + (2 if k == 1 else 0)) % QUARTERS
 
@@ -303,7 +306,7 @@
                     if source == done:
                         section_copy(k, index).start()
 
-    for step in list(range(STEPS_DEV // 2, STEPS_DEV)) + list(range(STEPS_DEV // 2)):
+    for step in range(STEPS_DEV):
         to = moved(me, step, 1)
         outgoing[step] = pack([ids[to, i] for i in range(CAP)])
         region_copy(step).start()
@@ -311,13 +314,14 @@
     row = lax.broadcasted_iota(jnp.int32, (128, 128), 0)
     column = lax.broadcasted_iota(jnp.int32, (128, 128), 1)
     origin = jnp.full((128, 128), -2, jnp.int32)
-    local = jnp.zeros((8, 128), jnp.bool_)
     for step in range(STEPS_DEV):
         origin = jnp.where(row == step, moved(me, step, -1), origin)
-        local = jnp.logical_or(local, jnp.broadcast_to(device, (8, 128)) == moved(me, step, -1))
+        if step != MUTUAL:
+            origin = jnp.where(row == STEPS_DEV + step, moved(me, step, 1), origin)
+    sign = jnp.where(row < STEPS_DEV, 1.0, -1.0)
     for i in range(CAP):
         chosen = jnp.logical_and(origin == device, rank == i)
-        from_slot[:, 128 * i : 128 * i + 128] = chosen.astype(F32).astype(BF16)
+        from_slot[:, 128 * i : 128 * i + 128] = jnp.where(chosen, sign, 0.0).astype(BF16)
         chosen = CAP * row + i == column
         chosen = jnp.logical_and(chosen, column < WIN_DEV)
         from_group[:, 128 * i : 128 * i + 128] = chosen.astype(F32).astype(BF16)
@@ -347,17 +351,33 @@
         backs[QROWS * u : QROWS * u + QROWS, :256] = back[:QROWS]
         backs[QROWS * u : QROWS * u + QROWS, 256:] = back[QROWS:]
 
-    def weigh(rows):
+    column_value = (lane % TLANES - RADIUS).astype(F32)
+    lane8 = lane_iota(8)
+    row8 = lax.broadcasted_iota(jnp.int32, (8, 128), 0)
+
+    def weigh():
         surfaces = jnp.dot(backs[...], back_right_ref[...], preferred_element_type=F32)
         energies = exact_dot(squares[...], energy_ref[...]) / (WIN * WIN)
-        for u, row in enumerate(rows):
+        for u in range(CHUNK):
             first = jnp.sum(energies[16 * u : 16 * u + 8], axis=0, keepdims=True)
             second = jnp.sum(energies[16 * u + 8 : 16 * u + 16], axis=0, keepdims=True)
             norm = jnp.sqrt(first * second + 1e-06)
             surface = surfaces[QROWS * u : QROWS * u + QROWS]
             weights = jnp.where(shift_mask, jnp.exp(sharpness * (surface / norm)), 0.0)
-            sums[0, pl.ds(row, 1), :] = jnp.sum(weights, axis=0, keepdims=True)
-            sums[1, pl.ds(row, 1), :] = jnp.sum(weights * row_value, axis=0, keepdims=True)
+            total = jnp.sum(weights, axis=0, keepdims=True)
+            sums[u : u + 1, :] = total
+            sums[8 + u : 9 + u, :] = jnp.sum(weights * row_value, axis=0, keepdims=True)
+            sums[16 + u : 17 + u, :] = total * column_value
+        parts = [
+            lax.dot_general(
+                member_ref[...], part, (((1,), (1,)), ((), ())), preferred_element_type=F32
+            )
+            for part in split3(sums[...])
+        ]
+        total = parts[0] + parts[1] + parts[2]
+        moment = jnp.where(row8 < CAP, pltpu.roll(total, 128 - 8, 1), pltpu.roll(total, 128 - 16, 1))
+        flows = moment / jnp.where(total == 0.0, 1.0, total)
+        return jnp.where(jnp.logical_and(jnp.abs(flows) <= 2.0 * RADIUS, lane8 < CHUNK), flows, 0.0)
 
     def section_batch(chunk, _):
         pltpu.make_async_remote_copy(
@@ -371,72 +391,61 @@
         first = CHUNK * ((SHARE // CHUNK * sec + chunk) % QUARTERS)
         for u in range(CHUNK):
             correlate(natural.at[first + u], from_section.at[CHUNK * chunk + u], u)
-        weigh([STEPS_DEV + CHUNK * chunk + u for u in range(CHUNK)])
+        flows = weigh()
+        flows = jnp.where(chunk < sec, -flows, flows)
+        sections[...] += pltpu.roll(flows, CHUNK * chunk, 1)
         return 0
 
-    def region_batch(batch, _):
+    def early_copy(step):
+        return pltpu.make_async_remote_copy(
+            src_ref=published.at[0],
+            dst_ref=early.at[step],
+            send_sem=early_send,
+            recv_sem=early_recv,
+            device_id={"region": moved(me, step, -1)},
+            device_id_type=MESH,
+        )
+
+    def late_copy(step, k):
+        return pltpu.make_async_remote_copy(
+            src_ref=published.at[1],
+            dst_ref=late.at[step - EARLY, sec],
+            send_sem=late_send,
+            recv_sem=late_recv,
+            device_id={"sec": k, "region": moved(me, step, -1)},
+            device_id_type=MESH,
+        )
+
+    def ours_copy(d):
+        return pltpu.make_async_remote_copy(
+            src_ref=ours.at[0],
+            dst_ref=ours.at[d],
+            send_sem=ours_send,
+            recv_sem=ours_recv,
+            device_id={"sec": (sec + d) % SECTIONS},
+            device_id_type=MESH,
+        )
+
+    def field_copy(o):
+        return pltpu.make_async_remote_copy(
+            src_ref=field,
+            dst_ref=fields.at[REGIONS - 1 - o],
+            send_sem=field_send,
+            recv_sem=field_recv,
+            device_id=neighbour(o),
+            device_id_type=MESH,
+        )
+
+    def region_batch(batch):
         for u in range(CHUNK):
             step = CHUNK * batch + u
-            packed[u] = pack([local_ids[CAP * step + i] for i in range(CAP)])
-            pltpu.make_async_remote_copy(
-                src_ref=outgoing.at[0],
-                dst_ref=from_region.at[step],
-                send_sem=reg_send.at[step],
-                recv_sem=reg_recv.at[step],
-                device_id=neighbour(1),
-                device_id_type=MESH,
-            ).wait_recv()
+            origin = moved(me, step, -1)
+            packed[u] = pack([ids[origin, i] for i in range(CAP)])
+            region_copy(step).wait_recv()
             correlate(packed.at[u], from_region.at[step], u)
-        weigh([CHUNK * batch + u for u in range(CHUNK)])
-        return 0
-
-    batches = STEPS_DEV // CHUNK
-    lax.fori_loop(0, batches // 2, region_batch, 0)
-    lax.fori_loop(0, SHARE // CHUNK, section_batch, 0)
-    lax.fori_loop(batches // 2, batches, region_batch, 0)
-
-    nt = (((1,), (1,)), ((), ()))
-
-    def turned(table, x):
-        parts = [
-            lax.dot_general(table, part, nt, preferred_element_type=F32) for part in split3(x)
-        ]
-        return parts[0] + parts[1] + parts[2]
-
-    column_value = (lane % TLANES - RADIUS).astype(F32)
-    total = turned(member_ref[0] + member_ref[1], sums[0])
-    moment = turned(member_ref[0], sums[1]) + turned(member_ref[1], sums[0] * column_value)
-    flows = moment / jnp.where(total == 0.0, 1.0, total)
-    lane8 = lane_iota(8)
-    swapped = jnp.logical_and(lane8 >= STEPS_DEV, lane8 < STEPS_DEV + CHUNK * sec)
-    flows = jnp.where(swapped, -flows, flows)
-    flows = jnp.where(jnp.abs(flows) <= 2.0 * RADIUS, flows, 0.0)
-    mine[...] = flows
-
-    def p1_copy(d):
-        return pltpu.make_async_remote_copy(
-            src_ref=mine,
-            dst_ref=gathered.at[d - 1],
-            send_sem=p1_send.at[d - 1],
-            recv_sem=p1_recv.at[d - 1],
-            device_id={"sec": (sec + d) % SECTIONS},
-            device_id_type=MESH,
-        )
-
-    for d in range(1, SECTIONS):
-        p1_copy(d).start()
-    for d in range(1, SECTIONS):
-        p1_copy(d).wait_recv()
-    blocks = []
-    section = jnp.zeros((8, 128), F32)
-    for k in range(SECTIONS):
-        block = flows
-        for d in range(1, SECTIONS):
-            block = jnp.where((sec - k + SECTIONS) % SECTIONS == d, gathered[d - 1], block)
-        blocks.append(block)
-        turned_block = pltpu.roll(block, (SHARE * k - STEPS_DEV + 128) % 128, 1)
-        here = jnp.logical_and(lane8 >= SHARE * k, lane8 < SHARE * k + SHARE)
-        section = jnp.where(here, turned_block, section)
+        flows = weigh()
+        flows += pltpu.roll(flows, STEPS_DEV, 1)
+        return pltpu.roll(flows, CHUNK * batch, 1) if batch else flows
 
     def by_window(x, table):
         spread = exact_dot(x, table)
@@ -449,48 +458,75 @@
                 )
         return rows
 
-    edges = [section] + [
-        pltpu.roll(section, 128 - GROUPS * e, 1) for e in range(1, SECTIONS - 1)
-    ]
+    sections[...] = jnp.zeros((8, 128), F32)
+    flows = region_batch(0) + region_batch(1)
+    lax.fori_loop(0, SHARE // CHUNK, section_batch, 0)
+    section = sections[...]
+    shift = section
+    for k in range(1, SECTIONS):
+        shift = jnp.where(sec == k, pltpu.roll(section, SHARE * k, 1), shift)
+    edges = [shift] + [pltpu.roll(shift, 128 - GROUPS * e, 1) for e in range(1, SECTIONS - 1)]
     edges = [jnp.where(lane8 < GROUPS, edge, 0.0) for edge in edges]
-    blocks = [jnp.where(lane8 < STEPS_DEV, block, 0.0) for block in blocks]
-    montage_rows = by_window(jnp.concatenate(blocks, axis=0), from_slot[...])
     section_rows = by_window(jnp.concatenate(edges, axis=0), from_group[...])
-    montage = jnp.concatenate(montage_rows, axis=0)
     section = jnp.concatenate(section_rows + [jnp.zeros((2, 128), F32)], axis=0)
-    field[0:8, :] = montage
-    field[8:16, :] = section
-
-    def p2_copy(o):
-        return pltpu.make_async_remote_copy(
-            src_ref=field,
-            dst_ref=fields.at[REGIONS - o],
-            send_sem=p2_send.at[o - 1],
-            recv_sem=p2_recv.at[REGIONS - 1 - o],
-            device_id=neighbour(o),
-            device_id_type=MESH,
-        )
-
-    def p2_start(o, _):
-        p2_copy(o).start()
+    field[...] = section
+
+    def field_start(o, _):
+        field_copy(o).start()
         return 0
 
-    def p2_wait(o, _):
-        p2_copy(o).wait_recv()
-        return 0
-
-    lax.fori_loop(1, REGIONS, p2_start, 0)
-    lax.fori_loop(1, REGIONS, p2_wait, 0)
-
-    theirs = exact_dot(fields[1:].reshape(16 * (REGIONS - 1), 128), from_partner[...])
-    partner_field = jnp.zeros((16, 128), F32)
+    lax.fori_loop(1, REGIONS, field_start, 0)
+    pl.semaphore_wait(ready, SECTIONS - 1)
+    flows += region_batch(2)
+    published[0] = flows
+    for step in range(EARLY):
+        early_copy(step).start()
+    flows += region_batch(3)
+    published[1] = flows
+    for step in range(EARLY, STEPS_DEV):
+        for k in range(SECTIONS):
+            late_copy(step, k).start()
+
+    pltpu.make_async_copy(fields, fields, field_recv).wait()
+    found = exact_dot(fields[...].reshape(8 * (REGIONS - 1), 128), from_partner[...])
+    partner_section = jnp.zeros((8, 128), F32)
     for o in range(1, REGIONS):
-        here = jnp.broadcast_to(device, (16, 128)) == (me + o) % REGIONS
-        partner_field = jnp.where(here, theirs[16 * o - 16 : 16 * o], partner_field)
-    montage = jnp.where(local, montage, -partner_field[:8])
-    partner_section = partner_field[8:]
-
-    row8 = lax.broadcasted_iota(jnp.int32, (8, 128), 0)
+        here = jnp.broadcast_to(device, (8, 128)) == (me + o) % REGIONS
+        partner_section = jnp.where(here, found[8 * o - 8 : 8 * o], partner_section)
+    pltpu.make_async_copy(early, early, early_recv).wait()
+    for step in range(EARLY):
+        flows = jnp.where(lane8 == STEPS_DEV + step, early[step], flows)
+    ours[0, 0:8, :] = flows
+    ours[0, 8:16, :] = section
+    ours[0, 16:24, :] = partner_section
+    for d in range(1, SECTIONS):
+        ours_copy(d).start()
+    for k in range(SECTIONS):
+
+        @pl.when(sec == k)
+        def _():
+            for index in range(len(section_sends(k))):
+                section_copy(k, index).wait_send()
+
+    for step in range(STEPS_DEV):
+        region_copy(step).wait_send()
+    pltpu.make_async_copy(fields, fields, field_send).wait()
+    pltpu.make_async_copy(early, early, early_send).wait()
+    pltpu.make_async_copy(late, late, late_recv).wait()
+    others = ours.at[pl.ds(1, SECTIONS - 1)]
+    pltpu.make_async_copy(others, others, ours_recv).wait()
+    blocks = []
+    for k in range(SECTIONS):
+        block = ours[(sec - k + SECTIONS) % SECTIONS, 0:8, :]
+        for step in range(EARLY, STEPS_DEV):
+            block = jnp.where(lane8 == STEPS_DEV + step, late[step - EARLY, k], block)
+        blocks.append(block)
+    montage = jnp.concatenate(
+        by_window(jnp.concatenate(blocks, axis=0), from_slot[...]), axis=0
+    )
+    section = ours[0, 8:16, :] + ours[1, 8:16, :] + ours[2, 8:16, :] + ours[3, 8:16, :]
+    partner_section = ours[0, 16:24, :] + ours[1, 16:24, :] + ours[2, 16:24, :] + ours[3, 16:24, :]
+
     has_next = jnp.where(row8 < 2 * (SECTIONS - 1), 1.0, 0.0)
     has_prev = jnp.where(row8 >= 2, 1.0, 0.0)
     disagreement = 2.0 * montage
@@ -528,23 +564,8 @@
         out_ref[2 * k : 2 * k + 2, :] = chosen
     out_ref[6:8, :] = jnp.zeros((2, 128), F32)
 
-    for k in range(SECTIONS):
-
-        @pl.when(sec == k)
-        def _():
-            for index in range(len(section_sends(k))):
-                section_copy(k, index).wait_send()
-
-    for step in range(STEPS_DEV):
-        region_copy(step).wait_send()
-    for d in range(1, SECTIONS):
-        p1_copy(d).wait_send()
-
-    def p2_sent(o, _):
-        p2_copy(o).wait_send()
-        return 0
-
-    lax.fori_loop(1, REGIONS, p2_sent, 0)
+    pltpu.make_async_copy(late, late, late_send).wait()
+    pltpu.make_async_copy(others, others, ours_send).wait()
 
 
 def split_kernel(rows_ref, montage_ref, section_ref, shift_ref):
@@ -570,7 +591,7 @@
             pltpu.VMEM((2 * QROWS, 2 * WIN), BF16),
             pltpu.VMEM((512, 128), BF16),
             pltpu.VMEM((256, 128), BF16),
-            pltpu.VMEM((2, 8, 128), BF16),
+            pltpu.VMEM((8, 128), BF16),
             pltpu.VMEM((WIN_DEV, WIN * WIN), BF16),
             pltpu.VMEM((WIN * WIN_DEV, 128), F32),
             pltpu.VMEM((WIN * WIN_DEV, 128), F32),
@@ -583,29 +604,36 @@
             pltpu.VMEM((CHUNK,) + side, BF16),
             pltpu.VMEM((CHUNK * QROWS, 512), BF16),
             pltpu.VMEM((CHUNK * 16, 256), F32),
-            pltpu.VMEM((2, 128, 128), F32),
+            pltpu.VMEM((128, 128), F32),
             pltpu.VMEM((1, 128), jnp.int32),
             pltpu.VMEM((1, 128), jnp.int32),
             pltpu.VMEM((REGIONS, 128), jnp.int32),
             pltpu.SMEM((REGIONS, 128), jnp.int32),
-            pltpu.SMEM((CAP * STEPS_DEV,), jnp.int32),
             pltpu.VMEM((128, CAP * 128), BF16),
             pltpu.VMEM((128, CAP * 128), BF16),
             pltpu.VMEM((128, 128), BF16),
-            pltpu.VMEM((SECTIONS - 1, 8, 128), F32),
+            pltpu.VMEM((2, 8, 128), F32),
+            pltpu.VMEM((SECTIONS, 24, 128), F32),
+            pltpu.VMEM((EARLY, 8, 128), F32),
+            pltpu.VMEM((STEPS_DEV - EARLY, SECTIONS, 8, 128), F32),
             pltpu.VMEM((8, 128), F32),
-            pltpu.VMEM((16, 128), F32),
-            pltpu.VMEM((REGIONS, 16, 128), F32),
+            pltpu.VMEM((8, 128), F32),
+            pltpu.VMEM((REGIONS - 1, 8, 128), F32),
             dma((PARTS + 6,)),
             dma,
             dma((5,)),
             dma((SHARE // CHUNK,)),
             dma((STEPS_DEV,)),
             dma((STEPS_DEV,)),
-            dma((SECTIONS - 1,)),
-            dma((SECTIONS - 1,)),
-            dma((REGIONS - 1,)),
-            dma((REGIONS - 1,)),
+            dma,
+            dma,
+            dma,
+            dma,
+            dma,
+            dma,
+            dma,
+            dma,
+            pltpu.SemaphoreType.REGULAR,
         ],
         compiler_params=pltpu.CompilerParams(
             vmem_limit_bytes=60 << 20, collective_id=0, has_side_effects=True

time: 73.3 us -> 70.7 us (0.965)
  Pallas kernels: 72.5 us -> 69.9 us
    pallas_call x1, Pallas kernels: 71.3 us -> 68.6 us  [body(): pl.pallas_call(flow_kernel, out_shape=jax.ShapeDtypeStruct((8, 128), F32)...]
where the time goes in v3:
time: 70.7 us; the launch traced here: 70.5 us
  Pallas kernels  69.9 us (99%)
    pallas_call x1, Pallas kernels, body(): pl.pallas_call(flow_kernel, out_shape=jax.ShapeDtypeStruct((8, 128), F32)...  68.6 us

profile of v3, /device:TPU:1, one launch (start us, length us, event | category | flops | bytes accessed | tf_op | source)
XLA Modules:
  0.0 70.5 jit_solution(16043100284117670240)
XLA Ops:
  0.6 68.6 %flows.1.rows_ref = f32[8,128]{1,0:T(8,128)} custom-call(bf16[1,48,25600]{2,1,0:T(8,128)(2,1)} %win_hbm.1, s32[48]{0:T(128)} %dev_ref.1, s32[48]{0:T(128)} %slot_ref.1, bf16[4,256,256]{2,1,0:T(8,128)(2,1)} %constant.12.clone.right_hbm, bf16[320,320]{1,0:T(8,128)(2,1)} %constant.13.clone.left_hbm, bf16[96,320]{1,0:T(8,128)(2,1)} %constant.14.clone.back_left_hbm, ...), custom_call_target="tpu_custom_call" | custom-call | tf_op jit(solution)/shard_map/flows/pallas_call | solution.py:583
  69.2 1.3 %split.1 = (f32[1,2,48]{2,1,0:T(2,128)}, f32[1,2,48]{2,1,0:T(2,128)}, f32[1,2,48]{2,1,0:T(2,128)}) custom-call(f32[8,128]{1,0:T(8,128)} %flows.1.rows_ref), custom_call_target="tpu_custom_call" | custom-call | tf_op jit(solution)/shard_map/split/pallas_call | solution.py:644

commit v4 on v3

--- a/solution.py
+++ b/solution.py
@@ -28,7 +28,8 @@
 QUARTER = WIN // PHASES
 PARTS = 5
 STEPS_DEV = REGIONS // 2
-EARLY = STEPS_DEV - CHUNK
+EARLY = STEPS_DEV - 2
+BATCH = 6
 QUARTERS = GROUPS // CHUNK
 
 sharpness = 12.0
@@ -112,8 +113,8 @@
 
 
 STEPS = (
-    (1, 0, 0), (1, 0, 1), (-1, 0, 1), (1, 0, 2), (0, 0, 1), (2, 0, -1), "y", (0, 0, 2),
-    (-1, 1, 0), (-1, 1, -1), (1, 1, -1), (-1, 1, 2), (0, 1, -1), (2, 1, 1), "x", "xz",
+    (0, 0, 2), (1, 0, 2), "y", (0, 0, 1), (2, 0, -1), (1, 0, 0), (-1, 0, 1), (1, 0, 1),
+    (1, 1, -1), (2, 1, 1), (-1, 1, -1), "xz", (-1, 1, 0), (0, 1, -1), (-1, 1, 2), "x",
 )
 MUTUAL = STEPS.index((0, 0, 2))
 
@@ -156,18 +157,6 @@
     def neighbour(o):
         return {"region": (me + o) % REGIONS}
 
-    barrier = pltpu.get_barrier_semaphore()
-
-    def greet(o, _):
-        pl.semaphore_signal(barrier, inc=1, device_id=neighbour(o), device_id_type=MESH)
-        return 0
-
-    lax.fori_loop(1, REGIONS, greet, 0)
-    for d in range(1, SECTIONS):
-        pl.semaphore_signal(
-            barrier, inc=1, device_id={"sec": (sec + d) % SECTIONS}, device_id_type=MESH
-        )
-
     width = WIN * WIN // PARTS
     load_right = pltpu.make_async_copy(right_hbm, right_ref, load_sem.at[PARTS])
     load_tables = [
@@ -192,31 +181,20 @@
     load_right.start()
     for part in range(PARTS):
         load_part(part).start()
+
+    barrier = pltpu.get_barrier_semaphore()
+
+    def greet(o, _):
+        pl.semaphore_signal(barrier, inc=1, device_id=neighbour(o), device_id_type=MESH)
+        return 0
+
+    lax.fori_loop(1, REGIONS, greet, 0)
+    for d in range(1, SECTIONS):
+        pl.semaphore_signal(
+            barrier, inc=1, device_id={"sec": (sec + d) % SECTIONS}, device_id_type=MESH
+        )
     for load in load_tables:
         load.start()
-
-    lane = lane_iota()
-    dev_row[...] = jnp.full((1, 128), -1, jnp.int32)
-    slot_row[...] = jnp.full((1, 128), -1, jnp.int32)
-    dev_row[0:1, 0:WIN_DEV] = dev_ref[...].reshape(1, WIN_DEV)
-    slot_row[0:1, 0:WIN_DEV] = slot_ref[...].reshape(1, WIN_DEV)
-    device, partner = dev_row[...], slot_row[...]
-    code = jnp.where(me < device, lane, partner) * 64 + lane
-    same = device == lax.broadcasted_iota(jnp.int32, (REGIONS, 128), 0)
-    left_over = jnp.where(same, code, EMPTY)
-    rank = jnp.zeros((1, 128), jnp.int32)
-    listed = jnp.zeros((REGIONS, 128), jnp.int32)
-    lane32 = lane_iota(REGIONS)
-    for i in range(CAP):
-        least = jnp.min(left_over, axis=1, keepdims=True)
-        found = jnp.logical_and(same, left_over == least)
-        rank += i * jnp.sum(jnp.where(found, 1, 0), axis=0, keepdims=True)
-        window = jnp.where(least < EMPTY, least % 64, 0)
-        listed = jnp.where(lane32 == i, window, listed)
-        left_over = jnp.where(left_over > least, left_over, EMPTY)
-    ids_vmem[...] = listed
-    load_ids = pltpu.make_async_copy(ids_vmem, ids, ids_sem)
-    load_ids.start()
 
     load_right.wait()
     for part in range(PARTS):
@@ -234,7 +212,6 @@
             seg_im[start : start + 8 * WIN_DEV, :] = seg[:, 128:]
     for load in load_tables:
         load.wait()
-    load_ids.wait()
 
     wide = lane_iota(2 * WIN)
 
@@ -288,6 +265,7 @@
             natural[2 * part + k] = pack([w, w + 1, w + 2])
         return first
 
+    lane = lane_iota()
     start = jnp.where(sec == 1, 2, 0)
     for quarter in range(QUARTERS):
         lax.fori_loop(2 * quarter, 2 * quarter + 2, spectra_step, start)
@@ -305,6 +283,32 @@
                 for index, (_, source, _) in enumerate(section_sends(k)):
                     if source == done:
                         section_copy(k, index).start()
+
+        if quarter != 1:
+            continue
+        dev_row[...] = jnp.full((1, 128), -1, jnp.int32)
+        slot_row[...] = jnp.full((1, 128), -1, jnp.int32)
+        dev_row[0:1, 0:WIN_DEV] = dev_ref[...].reshape(1, WIN_DEV)
+        slot_row[0:1, 0:WIN_DEV] = slot_ref[...].reshape(1, WIN_DEV)
+        device, partner = dev_row[...], slot_row[...]
+        code = jnp.where(me < device, lane, partner) * 64 + lane
+        same = device == lax.broadcasted_iota(jnp.int32, (REGIONS, 128), 0)
+        left_over = jnp.where(same, code, EMPTY)
+        rank = jnp.zeros((1, 128), jnp.int32)
+        listed = jnp.zeros((REGIONS, 128), jnp.int32)
+        lane32 = lane_iota(REGIONS)
+        for i in range(CAP):
+            least = jnp.min(left_over, axis=1, keepdims=True)
+            found = jnp.logical_and(same, left_over == least)
+            rank += i * jnp.sum(jnp.where(found, 1, 0), axis=0, keepdims=True)
+            window = jnp.where(least < EMPTY, least % 64, 0)
+            listed = jnp.where(lane32 == i, window, listed)
+            left_over = jnp.where(left_over > least, left_over, EMPTY)
+        ids_vmem[...] = listed
+        load_ids = pltpu.make_async_copy(ids_vmem, ids, ids_sem)
+        load_ids.start()
+
+    load_ids.wait()
 
     for step in range(STEPS_DEV):
         to = moved(me, step, 1)
@@ -355,10 +359,12 @@
     lane8 = lane_iota(8)
     row8 = lax.broadcasted_iota(jnp.int32, (8, 128), 0)
 
-    def weigh():
-        surfaces = jnp.dot(backs[...], back_right_ref[...], preferred_element_type=F32)
-        energies = exact_dot(squares[...], energy_ref[...]) / (WIN * WIN)
-        for u in range(CHUNK):
+    def weigh(count):
+        surfaces = jnp.dot(
+            backs[: QROWS * count], back_right_ref[...], preferred_element_type=F32
+        )
+        energies = exact_dot(squares[: 16 * count], energy_ref[...]) / (WIN * WIN)
+        for u in range(count):
             first = jnp.sum(energies[16 * u : 16 * u + 8], axis=0, keepdims=True)
             second = jnp.sum(energies[16 * u + 8 : 16 * u + 16], axis=0, keepdims=True)
             norm = jnp.sqrt(first * second + 1e-06)
@@ -377,7 +383,7 @@
         total = parts[0] + parts[1] + parts[2]
         moment = jnp.where(row8 < CAP, pltpu.roll(total, 128 - 8, 1), pltpu.roll(total, 128 - 16, 1))
         flows = moment / jnp.where(total == 0.0, 1.0, total)
-        return jnp.where(jnp.logical_and(jnp.abs(flows) <= 2.0 * RADIUS, lane8 < CHUNK), flows, 0.0)
+        return jnp.where(jnp.logical_and(jnp.abs(flows) <= 2.0 * RADIUS, lane8 < count), flows, 0.0)
 
     def section_batch(chunk, _):
         pltpu.make_async_remote_copy(
@@ -391,7 +397,7 @@
         first = CHUNK * ((SHARE // CHUNK * sec + chunk) % QUARTERS)
         for u in range(CHUNK):
             correlate(natural.at[first + u], from_section.at[CHUNK * chunk + u], u)
-        flows = weigh()
+        flows = weigh(CHUNK)
         flows = jnp.where(chunk < sec, -flows, flows)
         sections[...] += pltpu.roll(flows, CHUNK * chunk, 1)
         return 0
@@ -436,16 +442,15 @@
             device_id_type=MESH,
         )
 
-    def region_batch(batch):
-        for u in range(CHUNK):
-            step = CHUNK * batch + u
+    def region_batch(first, last):
+        for u, step in enumerate(range(first, last)):
             origin = moved(me, step, -1)
             packed[u] = pack([ids[origin, i] for i in range(CAP)])
             region_copy(step).wait_recv()
             correlate(packed.at[u], from_region.at[step], u)
-        flows = weigh()
+        flows = weigh(last - first)
         flows += pltpu.roll(flows, STEPS_DEV, 1)
-        return pltpu.roll(flows, CHUNK * batch, 1) if batch else flows
+        return pltpu.roll(flows, first, 1) if first else flows
 
     def by_window(x, table):
         spread = exact_dot(x, table)
@@ -459,8 +464,13 @@
         return rows
 
     sections[...] = jnp.zeros((8, 128), F32)
-    flows = region_batch(0) + region_batch(1)
-    lax.fori_loop(0, SHARE // CHUNK, section_batch, 0)
+    chunks = SHARE // CHUNK
+    low = jnp.where(sec == 2, chunks - 1, 0)
+    high = jnp.where(sec == 1, 1, chunks)
+    lax.fori_loop(low, high, section_batch, 0)
+    flows = region_batch(0, 4)
+    lax.fori_loop(0, low, section_batch, 0)
+    lax.fori_loop(high, chunks, section_batch, 0)
     section = sections[...]
     shift = section
     for k in range(1, SECTIONS):
@@ -477,11 +487,12 @@
 
     lax.fori_loop(1, REGIONS, field_start, 0)
     pl.semaphore_wait(ready, SECTIONS - 1)
-    flows += region_batch(2)
+    flows += region_batch(4, 8)
+    flows += region_batch(8, EARLY)
     published[0] = flows
     for step in range(EARLY):
         early_copy(step).start()
-    flows += region_batch(3)
+    flows += region_batch(EARLY, STEPS_DEV)
     published[1] = flows
     for step in range(EARLY, STEPS_DEV):
         for k in range(SECTIONS):
@@ -598,12 +609,12 @@
             pltpu.VMEM((WIN_DEV, 2 * WIN, 128), BF16),
             pltpu.VMEM((GROUPS,) + side, BF16),
             pltpu.VMEM((STEPS_DEV,) + side, BF16),
-            pltpu.VMEM((CHUNK,) + side, BF16),
+            pltpu.VMEM((BATCH,) + side, BF16),
             pltpu.VMEM((SHARE,) + side, BF16),
             pltpu.VMEM((STEPS_DEV,) + side, BF16),
-            pltpu.VMEM((CHUNK,) + side, BF16),
-            pltpu.VMEM((CHUNK * QROWS, 512), BF16),
-            pltpu.VMEM((CHUNK * 16, 256), F32),
+            pltpu.VMEM((BATCH,) + side, BF16),
+            pltpu.VMEM((BATCH * QROWS, 512), BF16),
+            pltpu.VMEM((BATCH * 16, 256), F32),
             pltpu.VMEM((128, 128), F32),
             pltpu.VMEM((1, 128), jnp.int32),
             pltpu.VMEM((1, 128), jnp.int32),

time: 70.7 us -> 69.1 us (0.977)
  Pallas kernels: 69.9 us -> 68.3 us
    pallas_call x1, Pallas kernels: 68.6 us -> 67.1 us  [body(): pl.pallas_call(flow_kernel, out_shape=jax.ShapeDtypeStruct((8, 128), F32)...]
where the time goes in v4:
time: 69.1 us; the launch traced here: 69 us
  Pallas kernels  68.3 us (99%)
    pallas_call x1, Pallas kernels, body(): pl.pallas_call(flow_kernel, out_shape=jax.ShapeDtypeStruct((8, 128), F32)...  67.1 us

profile of v4, /device:TPU:1, one launch (start us, length us, event | category | flops | bytes accessed | tf_op | source)
XLA Modules:
  0.0 69.0 jit_solution(10774862884242070353)
XLA Ops:
  0.6 67.1 %flows.1.rows_ref = f32[8,128]{1,0:T(8,128)} custom-call(bf16[1,48,25600]{2,1,0:T(8,128)(2,1)} %win_hbm.1, s32[48]{0:T(128)} %dev_ref.1, s32[48]{0:T(128)} %slot_ref.1, bf16[4,256,256]{2,1,0:T(8,128)(2,1)} %constant.12.clone.right_hbm, bf16[320,320]{1,0:T(8,128)(2,1)} %constant.13.clone.left_hbm, bf16[96,320]{1,0:T(8,128)(2,1)} %constant.14.clone.back_left_hbm, ...), custom_call_target="tpu_custom_call" | custom-call | tf_op jit(solution)/shard_map/flows/pallas_call | solution.py:594
  67.7 1.3 %split.1 = (f32[1,2,48]{2,1,0:T(2,128)}, f32[1,2,48]{2,1,0:T(2,128)}, f32[1,2,48]{2,1,0:T(2,128)}) custom-call(f32[8,128]{1,0:T(8,128)} %flows.1.rows_ref), custom_call_target="tpu_custom_call" | custom-call | tf_op jit(solution)/shard_map/split/pallas_call | solution.py:655

commit v5 on v4

--- a/solution.py
+++ b/solution.py
@@ -310,7 +310,8 @@
 
     load_ids.wait()
 
-    for step in range(STEPS_DEV):
+    across = STEPS_DEV // 2
+    for step in [n + k for n in range(across) for k in (across, 0)]:
         to = moved(me, step, 1)
         outgoing[step] = pack([ids[to, i] for i in range(CAP)])
         region_copy(step).start()

time: 69.1 us -> 69.1 us (level)
  no operation moved by 1% of the time
where the time goes in v5:
time: 69.1 us; the launch traced here: 69 us
  Pallas kernels  68.3 us (99%)
    pallas_call x1, Pallas kernels, body(): pl.pallas_call(flow_kernel, out_shape=jax.ShapeDtypeStruct((8, 128), F32)...  67.1 us

profile of v5, /device:TPU:1, one launch (start us, length us, event | category | flops | bytes accessed | tf_op | source)
XLA Modules:
  0.0 69.0 jit_solution(16689953182977074134)
XLA Ops:
  0.6 67.1 %flows.1.rows_ref = f32[8,128]{1,0:T(8,128)} custom-call(bf16[1,48,25600]{2,1,0:T(8,128)(2,1)} %win_hbm.1, s32[48]{0:T(128)} %dev_ref.1, s32[48]{0:T(128)} %slot_ref.1, bf16[4,256,256]{2,1,0:T(8,128)(2,1)} %constant.12.clone.right_hbm, bf16[320,320]{1,0:T(8,128)(2,1)} %constant.13.clone.left_hbm, bf16[96,320]{1,0:T(8,128)(2,1)} %constant.14.clone.back_left_hbm, ...), custom_call_target="tpu_custom_call" | custom-call | tf_op jit(solution)/shard_map/flows/pallas_call | solution.py:595
  67.7 1.3 %split.1 = (f32[1,2,48]{2,1,0:T(2,128)}, f32[1,2,48]{2,1,0:T(2,128)}, f32[1,2,48]{2,1,0:T(2,128)}) custom-call(f32[8,128]{1,0:T(8,128)} %flows.1.rows_ref), custom_call_target="tpu_custom_call" | custom-call | tf_op jit(solution)/shard_map/split/pallas_call | solution.py:656

commit v6 on v5

--- a/solution.py
+++ b/solution.py
@@ -268,7 +268,7 @@
     lane = lane_iota()
     start = jnp.where(sec == 1, 2, 0)
     for quarter in range(QUARTERS):
-        lax.fori_loop(2 * quarter, 2 * quarter + 2, spectra_step, start)
+        lax.fori_loop(2 * quarter, 2 * quarter + 2, spectra_step, start, unroll=True)
         if quarter == 0:
             pl.semaphore_wait(barrier, REGIONS - 1 + SECTIONS - 1)
             for d in range(1, SECTIONS):

time: 69.1 us -> 68.9 us (level)
  no operation moved by 1% of the time
where the time goes in v6:
time: 68.9 us; the launch traced here: 68.7 us
  Pallas kernels  68.1 us (99%)
    pallas_call x1, Pallas kernels, body(): pl.pallas_call(flow_kernel, out_shape=jax.ShapeDtypeStruct((8, 128), F32)...  66.8 us

profile of v6, /device:TPU:1, one launch (start us, length us, event | category | flops | bytes accessed | tf_op | source)
XLA Modules:
  0.0 68.7 jit_solution(9844781515873384809)
XLA Ops:
  0.6 66.8 %flows.1.rows_ref = f32[8,128]{1,0:T(8,128)} custom-call(bf16[1,48,25600]{2,1,0:T(8,128)(2,1)} %win_hbm.1, s32[48]{0:T(128)} %dev_ref.1, s32[48]{0:T(128)} %slot_ref.1, bf16[4,256,256]{2,1,0:T(8,128)(2,1)} %constant.12.clone.right_hbm, bf16[320,320]{1,0:T(8,128)(2,1)} %constant.13.clone.left_hbm, bf16[96,320]{1,0:T(8,128)(2,1)} %constant.14.clone.back_left_hbm, ...), custom_call_target="tpu_custom_call" | custom-call | tf_op jit(solution)/shard_map/flows/pallas_call | solution.py:595
  67.5 1.3 %split.1 = (f32[1,2,48]{2,1,0:T(2,128)}, f32[1,2,48]{2,1,0:T(2,128)}, f32[1,2,48]{2,1,0:T(2,128)}) custom-call(f32[8,128]{1,0:T(8,128)} %flows.1.rows_ref), custom_call_target="tpu_custom_call" | custom-call | tf_op jit(solution)/shard_map/split/pallas_call | solution.py:656
